TPU v7x, 128 devices: a whole 4x4x4 slice. The times are simulated.
128 devices in a mesh: ctx: 32 (over x, z, core), tp: 2 (over y_lo), dp: 2 (over y_hi).
Axes of the slice: x: 4, y: 4 (y_hi: 2, y_lo: 2; y = y_hi * 2 + y_lo), z: 4, core: 2. Of those that a mesh axis runs over, the one named last changes fastest.
Arguments:
- prompt_hidden: bfloat16 [2, 2048, 5120], P('dp', 'ctx'), may hold values from -6 to 6
- key_weight: bfloat16 [5120, 1024], P(None, 'tp'), may hold values from -0.078125 to 0.078125
- value_weight: bfloat16 [5120, 1024], P(None, 'tp'), may hold values from -0.078125 to 0.078125
- key_gain: float32 [128], replicated, may hold values from 0.1 to 1.9
- queries: bfloat16 [2, 3072, 8192], P('dp', 'ctx', 'tp'), may hold values from -100 to 100
- response_kv: bfloat16 [2, 3072, 2, 1024], P('dp', 'ctx', None, 'tp'), may hold values from -6 to 6
- targets: bfloat16 [2, 3072, 8192], P('dp', 'ctx', 'tp'), may hold values from -1.5 to 1.5
- ref_scores: float32 [2, 256], P('dp'), may hold values from -16 to 16
- lengths: int32 [2, 32, 8], P('dp', 'ctx'), may hold values from 1 to 48, 96 in all within a row
- placement_map: int32 [2, 256], P('dp', 'ctx'), may hold values from 0 to 255, each once within a row
Outputs:
- dpo_loss: float32 [2], P('dp')
- query_grad: bfloat16 [2, 3072, 8192], P('dp', 'ctx', 'tp')
- response_kv_grad: bfloat16 [2, 3072, 2, 1024], P('dp', 'ctx', None, 'tp')
- prompt_grad: bfloat16 [2, 2048, 5120], P('dp', 'ctx', 'tp')
- weight_grad: float32 [5120, 2, 1024], P(('ctx', 'dp'), None, 'tp')
Inputs may be any that keep to these rules, and one draw needn't show every extreme that they name: The 8 lengths of one device sum to 96. `placement_map`: each group's map names every response once; response p < 128 is the chosen one of pair p, response p + 128 its rejected one.
All inputs are finite; a program needn't handle non-finite values.
Results may differ from a plain program's by a relative error of at most 0.035.
Values may be sent and summed in bfloat16 or wider, within the bound.
A program may use at most 192 MiB of HBM per device.

v0:
```python
import math

import jax
import jax.numpy as jnp
from jax import lax
from jax.sharding import PartitionSpec as P

NORM_EPS = 1e-06
DPO_BETA = 0.5
MASK_FILL = -1e30


def split_pair(stacked, heads, head_width):
    row_count = stacked.shape[0]
    return (
        stacked[:, 0].reshape(row_count, heads, head_width),
        stacked[:, 1].reshape(row_count, heads, head_width),
    )


def block_size(row_count):
    size_now = row_count
    while size_now > 512 and size_now % 2 == 0:
        size_now = size_now // 2
    return size_now


def shards(
    prompt_hidden,
    key_weight,
    value_weight,
    key_gain,
    queries,
    response_kv,
    targets,
    ref_scores,
    lengths,
    placement_map,
):
    hidden = prompt_hidden[0]
    prompt_rows, model_width = hidden.shape
    head_width = key_gain.shape[0]
    kv_width = key_weight.shape[1]
    kv_heads = kv_width // head_width
    resp_rows = queries.shape[1]
    query_heads = queries.shape[2] // head_width
    grouped = query_heads // kv_heads
    slot_count = lengths.shape[2]
    responses = ref_scores.shape[1]
    pair_count = responses // 2
    qk_scale = 1.0 / math.sqrt(head_width)
    raw_keys = jnp.dot(hidden, key_weight, preferred_element_type=jnp.float32).reshape(
        prompt_rows, kv_heads, head_width
    )
    inv_rms = lax.rsqrt(jnp.mean(raw_keys * raw_keys, axis=-1, keepdims=True) + NORM_EPS)
    prompt_keys = (
        (raw_keys * inv_rms * key_gain).astype(jnp.bfloat16).reshape(prompt_rows, kv_width)
    )
    prompt_values = jnp.dot(hidden, value_weight, preferred_element_type=jnp.float32).astype(
        jnp.bfloat16
    )
    prompt_kv = jnp.stack([prompt_keys, prompt_values], axis=1)
    query_four = queries[0].reshape(resp_rows, kv_heads, grouped, head_width)
    resp_keys, resp_values = split_pair(response_kv[0], kv_heads, head_width)
    ends = jnp.cumsum(lengths[0, 0], dtype=jnp.int32)
    row_ids = lax.iota(jnp.int32, resp_rows)
    slot_ids = jnp.sum(
        (row_ids[:, None] >= ends[None, :]).astype(jnp.int32), axis=1, dtype=jnp.int32
    )
    same_slot = (slot_ids[:, None] == slot_ids[None, :]) & (row_ids[None, :] <= row_ids[:, None])
    slot_onehot = (slot_ids[:, None] == lax.iota(jnp.int32, slot_count)[None, :]).astype(
        jnp.float32
    )
    place_onehot = (placement_map[0][:, None] == lax.iota(jnp.int32, responses)[None, :]).astype(
        jnp.float32
    )

    def block_logits(key_block, keep_mask):
        logits = (
            jnp.einsum("rkgd,jkd->kgrj", query_four, key_block, preferred_element_type=jnp.float32)
            * qk_scale
        )
        if keep_mask is None:
            return logits
        return jnp.where(keep_mask, logits, MASK_FILL)

    def fold_stats(states, key_block, keep_mask):
        peak_old, totals = states
        logits = block_logits(key_block, keep_mask)
        peak_new = jnp.maximum(peak_old, jnp.max(logits, axis=-1))
        totals = totals * jnp.exp(peak_old - peak_new) + jnp.sum(
            jnp.exp(logits - peak_new[..., None]), axis=-1
        )
        return (peak_new, totals)

    def fold_values(summed, key_block, value_block, keep_mask, log_total):
        logits = block_logits(key_block, keep_mask)
        weights = jnp.exp(logits - log_total[..., None]).astype(jnp.bfloat16)
        return summed + jnp.einsum(
            "kgrj,jkd->kgrd", weights, value_block, preferred_element_type=jnp.float32
        )

    def scan_stats(states, key_flat):
        key_block = key_flat.reshape(key_flat.shape[0], kv_heads, head_width)
        return (fold_stats(states, key_block, None), None)

    stat_shape = (kv_heads, grouped, resp_rows)
    start_stats = (jnp.full(stat_shape, MASK_FILL, jnp.float32), jnp.zeros(stat_shape, jnp.float32))
    value_start = jnp.zeros(stat_shape + (head_width,), jnp.float32)
    prompt_total = prompt_rows * lax.axis_size("ctx")
    block_len = block_size(prompt_total)
    block_count = prompt_total // block_len
    gathered = lax.all_gather(prompt_kv, "ctx", axis=0, tiled=True)
    blocks = gathered.reshape(block_count, block_len, 2, kv_width)
    stats, unused = lax.scan(scan_stats, start_stats, blocks[:, :, 0])
    peak_final, totals = fold_stats(stats, resp_keys, same_slot)
    log_total = peak_final + jnp.log(totals)

    def scan_values(summed, block):
        key_block, value_block = split_pair(block, kv_heads, head_width)
        return (fold_values(summed, key_block, value_block, None, log_total), None)

    summed, unused = lax.scan(scan_values, value_start, blocks)
    summed = fold_values(summed, resp_keys, resp_values, same_slot, log_total)
    attended = summed.astype(jnp.bfloat16)
    attended_rows = jnp.transpose(attended, (2, 0, 1, 3))
    token_part = jnp.einsum(
        "rc,rc->r",
        attended_rows.reshape(resp_rows, query_heads * head_width),
        targets[0],
        preferred_element_type=jnp.float32,
    )
    slot_part = jnp.sum(token_part[:, None] * slot_onehot, axis=0)
    slot_total = lax.psum(slot_part, "tp")
    scores = lax.psum(jnp.sum(slot_total[:, None] * place_onehot, axis=0), "ctx")
    shifted = scores - ref_scores[0]
    margin = DPO_BETA * (shifted[:pair_count] - shifted[pair_count:])
    dpo_loss = jnp.sum(jax.nn.softplus(-margin))
    pair_grad = -DPO_BETA * jax.nn.sigmoid(-margin)
    score_grad = jnp.concatenate([pair_grad, -pair_grad])
    slot_grad = jnp.sum(place_onehot * score_grad[None, :], axis=1)
    row_grad = jnp.sum(slot_onehot * slot_grad[None, :], axis=1)
    out_grad = (
        (row_grad[:, None] * targets[0].astype(jnp.float32))
        .astype(jnp.bfloat16)
        .reshape(resp_rows, kv_heads, grouped, head_width)
    )
    row_dot = jnp.einsum(
        "rkgd,rkgd->kgr", attended_rows, out_grad, preferred_element_type=jnp.float32
    )

    def block_backward(key_block, value_block, keep_mask):
        logits = block_logits(key_block, keep_mask)
        probs = jnp.exp(logits - log_total[..., None])
        prob_grad = jnp.einsum(
            "rkgd,jkd->kgrj", out_grad, value_block, preferred_element_type=jnp.float32
        )
        logit_grad = (probs * (prob_grad - row_dot[..., None])).astype(jnp.bfloat16)
        part_query = jnp.einsum(
            "kgrj,jkd->kgrd", logit_grad, key_block, preferred_element_type=jnp.float32
        )
        key_term = (
            jnp.einsum("kgrj,rkgd->jkd", logit_grad, query_four, preferred_element_type=jnp.float32)
            * qk_scale
        )
        value_term = jnp.einsum(
            "kgrj,rkgd->jkd",
            probs.astype(jnp.bfloat16),
            out_grad,
            preferred_element_type=jnp.float32,
        )
        return (part_query, key_term, value_term)

    def scan_backward(query_acc, block):
        key_block, value_block = split_pair(block, kv_heads, head_width)
        part_query, key_term, value_term = block_backward(key_block, value_block, None)
        return (
            query_acc + part_query,
            jnp.stack([key_term, value_term], axis=1).reshape(block.shape[0], 2, kv_width),
        )

    query_start = jnp.zeros(stat_shape + (head_width,), jnp.float32)
    query_acc, term_blocks = lax.scan(scan_backward, query_start, blocks)
    term_full = term_blocks.reshape(prompt_total, 2, kv_width)
    self_query, self_key, self_value = block_backward(resp_keys, resp_values, same_slot)
    query_total = (query_acc + self_query) * qk_scale
    query_grad = (
        jnp.transpose(query_total, (2, 0, 1, 3))
        .reshape(resp_rows, query_heads * head_width)
        .astype(jnp.bfloat16)
    )
    response_kv_grad = (
        jnp.stack([self_key, self_value], axis=1)
        .reshape(resp_rows, 2, kv_width)
        .astype(jnp.bfloat16)
    )
    owned_grad = lax.psum_scatter(
        term_full.astype(jnp.bfloat16), "ctx", scatter_dimension=0, tiled=True
    ).astype(jnp.float32)
    gain_grad = key_gain * owned_grad[:, 0].reshape(prompt_rows, kv_heads, head_width)
    raw_grad = inv_rms * gain_grad - raw_keys * inv_rms * inv_rms * inv_rms * jnp.mean(
        raw_keys * gain_grad, axis=-1, keepdims=True
    )
    kv_grad_b = jnp.stack(
        [raw_grad.reshape(prompt_rows, kv_width), owned_grad[:, 1]], axis=1
    ).astype(jnp.bfloat16)
    contract = (((1,), (1,)), ((), ()))
    hidden_part = lax.dot_general(
        kv_grad_b[:, 0], key_weight, contract, preferred_element_type=jnp.float32
    )
    hidden_part = hidden_part + lax.dot_general(
        kv_grad_b[:, 1], value_weight, contract, preferred_element_type=jnp.float32
    )
    prompt_grad = lax.psum_scatter(
        hidden_part.astype(jnp.bfloat16), "tp", scatter_dimension=1, tiled=True
    )
    flat_grad = kv_grad_b.reshape(prompt_rows, 2 * kv_width)
    token_contract = (((0,), (0,)), ((), ()))
    product = lax.dot_general(hidden, flat_grad, token_contract, preferred_element_type=jnp.float32)
    weight_grad = lax.psum_scatter(
        product.reshape(
            model_width // lax.axis_size(("ctx", "dp")) * lax.axis_size(("ctx", "dp")), 2, kv_width
        ),
        ("ctx", "dp"),
        scatter_dimension=0,
        tiled=True,
    )
    return (
        dpo_loss[None],
        query_grad[None],
        response_kv_grad[None],
        prompt_grad[None],
        weight_grad,
    )


def solution(mesh):
    in_specs = (
        P("dp", "ctx", None),
        P(None, "tp"),
        P(None, "tp"),
        P(),
        P("dp", "ctx", "tp"),
        P("dp", "ctx", None, "tp"),
        P("dp", "ctx", "tp"),
        P("dp", None),
        P("dp", "ctx", None),
        P("dp", "ctx"),
    )
    out_specs = (
        P("dp"),
        P("dp", "ctx", "tp"),
        P("dp", "ctx", None, "tp"),
        P("dp", "ctx", "tp"),
        P(("ctx", "dp"), None, "tp"),
    )
    return jax.shard_map(shards, mesh=mesh, in_specs=in_specs, out_specs=out_specs, check_vma=False)
```

profile of v0, /device:TPU:1, one launch (start us, length us, event | category | flops | bytes accessed | tf_op | source)
XLA Modules:
  0.0 1360.7 jit_solution(7182237405277355094)
XLA Ops:
  7.2 7.9 copy.196
  15.1 3.6 fusion.35
  27.9 44.2 %all-gather.2.cloned.1.call-done = bf16[2048,2,512]{2,0,1:T(8,128)(2,1)} async-done(((bf16[64,2,512]{2,0,1:T(8,128)(2,1)}), bf16[2048,2,512]{2,0,1:T(8,128)(2,1)}) %all-gather.2.cloned.1.call-update) | async-done | bytes 4194320 | tf_op jit(solution)/shard_map/all_gather | solution.py:113
  72.1 7.3 copy.144
  82.5 4.2 copy.220
  86.6 33.8 %while.37 = (s32[]{:T(128)}, f32[4,8,96]{2,1,0:T(8,128)S(1)}, f32[4,8,96]{2,1,0:T(8,128)S(1)}, bf16[4,512,512]{1,2,0:T(8,128)(2,1)}, bf16[96,4,8,128]{3,0,2,1:T(8,128)(2,1)S(1)}, /*index=5*/s32[]{:T(128)}, s32[]{:T(128)}) while((s32[]{:T(128)}, f32[4,8,96]{2,1,0:T(8,128)S(1)}, f32[4,8,96]{2,1,0:T(8,128)S(1)}, ...), condition=%wide.region_6.7_spmd.clone, body=%wide.region_3.6_spmd.clone.sunk | while | flops 410532864 | bytes 15102052 | solution.py:115
  91.4 3.7 fusion.113
  99.8 3.7 fusion.113
  108.3 3.7 fusion.113
  116.7 3.7 fusion.113
  121.9 22.1 %while.38 = (s32[]{:T(128)}, f32[4,8,96,128]{3,2,1,0:T(8,128)}, bf16[4,512,2,512]{1,3,2,0:T(8,128)(2,1)}, bf16[96,4,8,128]{3,0,2,1:T(8,128)(2,1)S(1)}, f32[4,8,96]{2,1,0:T(8,128)S(1)}, /*index=5*/s32[]{:T(128)}, s32[]{:T(128)}) while((s32[]{:T(128)}, f32[4,8,96,128]{3,2,1,0:T(8,128)}, bf16[4,512,2,512]{1,3,2,0:T(8,128)(2,1)}, ...), condition=%wide.region_10.11_spmd.clone, body=%wide.region_9.10_spmd.clone.sunk | while | flops 810811392 | bytes 9187427 | solution.py:123
  127.8 4.5 select_add_fusion.4
  133.6 4.5 select_add_fusion.4
  139.5 4.5 select_add_fusion.4
  148.4 3.8 psum.14
  152.3 63.6 %psum.15 = f32[256]{0:T(256)S(1)} all-reduce(f32[256]{0:T(256)S(1)} %select_reduce_fusion.1), channel_id=1, replica_groups=mesh['ctx'=32,'tp'=2,'dp'=2] {'ctx'}, use_global_device_ids=true, to_apply=%region_14.15 | all-reduce | flops 256 | bytes 2048 | tf_op jit(solution)/shard_map/psum | solution.py:135
  222.1 74.5 %while.39 = (s32[]{:T(128)}, f32[4,8,96,128]{3,2,1,0:T(8,128)}, bf16[4,512,2,512]{3,1,0,2:T(8,128)(2,1)}, bf16[4,512,2,512]{1,3,2,0:T(8,128)(2,1)}, bf16[96,4,8,...) while((s32[]{:T(128)}, f32[4,8,96,128]{3,2,1,0:T(8,128)}, ...), condition=%wide.region_19.20_spmd.clone, body=%wide.region_18.19_spmd.clone.sunk | while | flops 2027683840 | bytes 110661848 | solution.py:183
  227.1 3.9 fusion.132
  231.0 4.2 select_add_fusion.5
  245.4 3.9 fusion.132
  249.3 4.6 select_add_fusion.5
  264.2 3.9 fusion.132
  268.1 4.6 select_add_fusion.5
  282.9 3.9 fusion.132
  286.8 4.6 select_add_fusion.5
  296.7 78.1 %reduce-scatter.3.cloned.1.call-done = bf16[64,2,512]{2,0,1:T(8,128)(2,1)} async-done(((bf16[2048,2,512]{2,0,1:T(8,128)(2,1)}), bf16[64,2,512]{2,0,1:T(8,128)(2,1)}) %reduce-scatter.3.cloned.1.call-update) | async-done | bytes 131088 | tf_op jit(solution)/shard_map/reduce_scatter | solution.py:197
  376.2 8.7 fusion.39
  384.8 30.9 %copy.167 = f32[5120,2,512]{2,1,0:T(2,128)} copy(f32[5120,2,512]{0,2,1:T(8,128)} %bitcast.259) | data formatting | bytes 41943040 | tf_op jit(solution)/shard_map/reshape | solution.py:221
  417.7 4.2 fusion.45
  421.9 5.2 fusion.24
  441.1 890.4 %all-reduce.3.cloned.1.call-done = f32[5120,2,512]{2,1,0:T(2,128)} async-done(((f32[5120,2,512]{2,1,0:T(2,128)}), f32[5120,2,512]{2,1,0:T(2,128)}) %all-reduce.3.cloned.1.call-update) | async-done | bytes 20971536
  1333.2 21.0 %reduce-scatter.5.cloned.1.call-done = bf16[64,2560]{1,0:T(8,128)(2,1)} async-done(((bf16[64,5120]{1,0:T(8,128)(2,1)}), bf16[64,2560]{1,0:T(8,128)(2,1)}) %reduce-scatter.5.cloned.1.call-update) | async-done | bytes 327696 | tf_op jit(solution)/shard_map/reduce_scatter | solution.py:214
  (218 shorter events, 110.4 us)
Async XLA Ops:
  7.2 8.0 copy-start
  7.2 64.9 %all-gather.2.cloned.1.call-start = ((), (), s32[]{:S(2)}) async-start(), calls=%async_computation.2 | async-start | bytes 4325376 | tf_op jit(solution)/shard_map/all_gather | solution.py:113
  15.1 4.0 copy-start.6
  19.2 2.9 copy-start.21
  21.0 3.3 copy-start.31
  21.0 3.7 copy-start.13
  22.0 352.9 %reduce-scatter.3.cloned.1.call-start = ((), (), s32[]{:S(2)}) async-start(), calls=%async_computation.3 | async-start | bytes 4325376 | tf_op jit(solution)/shard_map/reduce_scatter | solution.py:197
  24.3 55.1 %copy-start.17 = (bf16[96,4,128]{2,1,0:T(4,128)(2,1)}, bf16[96,4,128]{2,1,0:T(4,128)(2,1)S(1)}, u32[]{:S(2)}) copy-start(bf16[96,4,128]{2,1,0:T(4,128)(2,1)S(1)} %reshape_squeeze.16) | copy-start | bytes 294916
  24.5 119.4 %copy-start.19 = (bf16[96,4,128]{2,1,0:T(4,128)(2,1)}, bf16[96,4,128]{2,1,0:T(4,128)(2,1)S(1)}, u32[]{:S(2)}) copy-start(bf16[96,4,128]{2,1,0:T(4,128)(2,1)S(1)} %reshape_squeeze.17) | copy-start | bytes 294916
  27.9 92.9 %copy-start.4 = (f32[4,8,96,96]{2,3,1,0:T(8,128)}, f32[4,8,96,96]{2,3,1,0:T(8,128)S(1)}, u32[]{:S(2)}) copy-start(f32[4,8,96,96]{2,3,1,0:T(8,128)S(1)} %get-tuple-element.330) | copy-start | bytes 3538948
  121.9 22.1 %copy-start.9 = (bf16[4,8,96,96]{2,3,1,0:T(8,128)(2,1)S(1)}, bf16[4,8,96,96]{2,3,1,0:T(8,128)(2,1)}, u32[]{:S(2)}) copy-start(bf16[4,8,96,96]{2,3,1,0:T(8,128)(2,1)} %fusion.28) | copy-start | bytes 1769476
  144.0 3.5 copy-start.14
  144.0 4.1 copy-start.12
  147.1 5.0 copy-start.28
  147.1 68.7 %copy-start.29 = (f32[1,256]{1,0:T(1,128)S(1)}, f32[1,256]{1,0:T(1,128)}, u32[]{:S(2)}) copy-start(f32[1,256]{1,0:T(1,128)} %param.23) | copy-start | bytes 3076
  231.0 4.2 copy-start.2
  249.3 4.6 copy-start.2
  268.1 4.6 copy-start.2
  286.8 4.6 copy-start.2
  291.4 2.8 copy-start.3
  296.6 79.2 %copy-start.16 = (f32[64,4,128]{2,0,1:T(8,128)S(1)}, f32[64,4,128]{2,0,1:T(8,128)}, u32[]{:S(2)}) copy-start(f32[64,4,128]{2,0,1:T(8,128)} %copy-done.15) | copy-start | bytes 393220
  296.6 79.2 %copy-start.27 = (f32[128]{0:T(128)S(1)}, f32[128]{0:T(128)}, u32[]{:S(2)}) copy-start(f32[128]{0:T(128)} %param.19) | copy-start | bytes 1540
  296.6 79.3 %copy-start.25 = (f32[64,4]{0,1:T(4,128)S(1)}, f32[64,4]{0,1:T(4,128)}, u32[]{:S(2)}) copy-start(f32[64,4]{0,1:T(4,128)} %copy-done.24) | copy-start | bytes 3076
  296.6 1034.9 %all-reduce.3.cloned.1.call-start = ((), (), s32[]{:S(2)}) async-start(), calls=%async_computation.5 | async-start | bytes 41943040
  415.8 938.4 %reduce-scatter.5.cloned.1.call-start = ((), (), s32[]{:S(2)}) async-start(), calls=%async_computation.4 | async-start | bytes 983040 | tf_op jit(solution)/shard_map/reduce_scatter | solution.py:214
  417.6 4.2 copy-start.23
  421.9 5.2 copy-start.5
  421.9 5.2 copy-start.8
  421.9 5.2 copy-start.20
  427.1 4.7 copy-start.18
  433.9 3.9 copy-start.11
  435.1 5.4 copy-start.30
  (14 other events, 28.5 us)
Sparse Core Ops, SparseCore 0:
  22.1 49.9 all-gather.1
  296.8 78.0 reduce-scatter.2
  415.9 915.5 all-reduce.2
  1334.4 19.7 reduce-scatter.4
where the time goes:
time: 1360 us
  waiting for transfers between devices  1030 us (76%)
  matrix products  117 us (9%)
  local copies, waits for them, and re-layouts  101 us (7%)
  blocking collectives  67.4 us (5%)
  other arithmetic  25 us (2%)
  between operations  15 us (1%)
    unnamed x5, waiting for transfers between devices  890 us
    reduce_scatter x1, waiting for transfers between devices, shards(): lax.psum_scatter(term_full.astype(jnp.bfloat16), 'ctx', scatter_dimension...  78.1 us
    psum x1, blocking collectives, shards(): lax.psum(jnp.sum(slot_total[:, None] * place_onehot, axis=0), 'ctx')  63.6 us
    all_gather x1, waiting for transfers between devices, shards(): gathered = lax.all_gather(prompt_kv, 'ctx', axis=0, tiled=True)  44.2 us
    reshape x1, local copies, waits for them, and re-layouts, shards(): product.reshape(model_width // lax.axis_size(('ctx', 'dp')) * lax.axis_si...  30.9 us
  transfers between devices with their start and end apart: 4, of which 4 were waited for; matrix products, arithmetic and copies ran while one was open for 2% of the time, Pallas kernels for 0%

commit v1 on v0

v1 whole, which is shorter than its diff:
```python
import functools
import math

import jax
import jax.numpy as jnp
from jax import lax
from jax.experimental import pallas as pl
from jax.experimental.pallas import tpu as pltpu
from jax.sharding import PartitionSpec as P

NORM_EPS = 1e-06
DPO_BETA = 0.5
MASK_FILL = -1e30
LOG2E = 1.4426950408889634
NT = (((1,), (1,)), ((), ()))
TN = (((0,), (0,)), ((), ()))
F32 = jnp.float32
BF16 = jnp.bfloat16


def attend_kernel(
    scale,
    q_ref,
    t_ref,
    k_ref,
    v_ref,
    rk_ref,
    rv_ref,
    bias_ref,
    e_ref,
    g_ref,
    er_ref,
    gr_ref,
    inv_ref,
    dq_ref,
    tok_ref,
):
    heads = q_ref.shape[1] // 128
    rows = q_ref.shape[0]
    q = jnp.concatenate([q_ref[:, i * 128 : (i + 1) * 128] for i in range(heads)], axis=0)
    t = jnp.concatenate([t_ref[:, i * 128 : (i + 1) * 128] for i in range(heads)], axis=0)
    bias = jnp.concatenate([bias_ref[...]] * heads, axis=0)
    k, v, rk, rv = k_ref[...], v_ref[...], rk_ref[...], rv_ref[...]
    s = lax.dot_general(q, k, NT, preferred_element_type=F32)
    sr = lax.dot_general(q, rk, NT, preferred_element_type=F32) + bias
    peak = jnp.maximum(
        jnp.max(s, axis=1, keepdims=True), jnp.max(sr, axis=1, keepdims=True)
    )
    factor = scale * LOG2E
    top = peak * factor
    e = jnp.exp2(s * factor - top)
    er = jnp.exp2(sr * factor - top)
    inv = 1.0 / (jnp.sum(e, axis=1, keepdims=True) + jnp.sum(er, axis=1, keepdims=True))
    eb, erb = e.astype(BF16), er.astype(BF16)
    e_ref[0] = eb
    er_ref[0] = erb
    attended = (
        jnp.dot(eb, v, preferred_element_type=F32) + jnp.dot(erb, rv, preferred_element_type=F32)
    ) * inv
    dot = jnp.sum(attended * t.astype(F32), axis=1, keepdims=True)
    dp = lax.dot_general(t, v, NT, preferred_element_type=F32)
    dpr = lax.dot_general(t, rv, NT, preferred_element_type=F32)
    gb = (e_ref[0].astype(F32) * (dp - dot)).astype(BF16)
    grb = (er_ref[0].astype(F32) * (dpr - dot)).astype(BF16)
    g_ref[0] = gb
    gr_ref[0] = grb
    dq = (
        jnp.dot(gb, k, preferred_element_type=F32) + jnp.dot(grb, rk, preferred_element_type=F32)
    ) * (inv * scale)
    inv_ref[0] = inv
    for i in range(heads):
        dq_ref[:, i * 128 : (i + 1) * 128] = dq[i * rows : (i + 1) * rows].astype(BF16)

    @pl.when((pl.program_id(0) == 0) & (pl.program_id(1) == 0))
    def _():
        tok_ref[...] = jnp.zeros_like(tok_ref)

    total = dot[:rows]
    for i in range(1, heads):
        total = total + dot[i * rows : (i + 1) * rows]
    tok_ref[...] += total


def attend(q, t, prompt_keys, prompt_values, rk, rv, bias, scale, grouped, chunk):
    rows = q.shape[0]
    tokens, kv_width = prompt_keys.shape
    kv_heads = kv_width // 128
    pad = rk.shape[0]
    steps = grouped // chunk
    m = chunk * rows
    total = grouped * rows
    row_block = pl.BlockSpec((rows, chunk * 128), lambda h, c: (0, h * steps + c))
    head_block = pl.BlockSpec((tokens, 128), lambda h, c: (0, h))
    resp_block = pl.BlockSpec((pad, 128), lambda h, c: (0, h))

    def score_block(width):
        return pl.BlockSpec((1, m, width), lambda h, c: (h, c, 0))

    return pl.pallas_call(
        functools.partial(attend_kernel, scale),
        grid=(kv_heads, steps),
        in_specs=[
            row_block,
            row_block,
            head_block,
            head_block,
            resp_block,
            resp_block,
            pl.BlockSpec((rows, pad), lambda h, c: (0, 0)),
        ],
        out_specs=[
            score_block(tokens),
            score_block(tokens),
            score_block(pad),
            score_block(pad),
            score_block(1),
            row_block,
            pl.BlockSpec((rows, 1), lambda h, c: (0, 0)),
        ],
        out_shape=[
            jax.ShapeDtypeStruct((kv_heads, total, tokens), BF16),
            jax.ShapeDtypeStruct((kv_heads, total, tokens), BF16),
            jax.ShapeDtypeStruct((kv_heads, total, pad), BF16),
            jax.ShapeDtypeStruct((kv_heads, total, pad), BF16),
            jax.ShapeDtypeStruct((kv_heads, total, 1), F32),
            jax.ShapeDtypeStruct(q.shape, BF16),
            jax.ShapeDtypeStruct((rows, 1), F32),
        ],
        compiler_params=pltpu.CompilerParams(vmem_limit_bytes=50 * 1024 * 1024),
        name="attend",
    )(q, t, prompt_keys, prompt_values, rk, rv, bias)


def keygrad_kernel(
    scale,
    e_ref,
    g_ref,
    er_ref,
    gr_ref,
    q_ref,
    t_ref,
    inv_ref,
    row_ref,
    dq_in_ref,
    dkv_ref,
    drkv_ref,
    dq_ref,
):
    heads = q_ref.shape[1] // 128
    rows = q_ref.shape[0]
    row_grad = row_ref[...]
    factor = inv_ref[0] * jnp.concatenate([row_grad] * heads, axis=0)
    q = jnp.concatenate([q_ref[:, i * 128 : (i + 1) * 128] for i in range(heads)], axis=0)
    t = jnp.concatenate([t_ref[:, i * 128 : (i + 1) * 128] for i in range(heads)], axis=0)
    qs = (q.astype(F32) * (factor * scale)).astype(BF16)
    ts = (t.astype(F32) * factor).astype(BF16)
    dkv_ref[0] = lax.dot_general(g_ref[0], qs, TN, preferred_element_type=F32).astype(BF16)
    dkv_ref[1] = lax.dot_general(e_ref[0], ts, TN, preferred_element_type=F32).astype(BF16)
    drkv_ref[0] = lax.dot_general(gr_ref[0], qs, TN, preferred_element_type=F32).astype(BF16)
    drkv_ref[1] = lax.dot_general(er_ref[0], ts, TN, preferred_element_type=F32).astype(BF16)
    dq_ref[...] = (dq_in_ref[...].astype(F32) * row_grad).astype(BF16)


def keygrad(e, g, er, gr, q, t, inv, row_grad, dq, scale):
    kv_heads, total, tokens = e.shape
    pad = er.shape[2]
    rows = q.shape[0]
    width = q.shape[1] // kv_heads

    def score_block(w):
        return pl.BlockSpec((1, total, w), lambda h: (h, 0, 0))

    row_block = pl.BlockSpec((rows, width), lambda h: (0, h))
    return pl.pallas_call(
        functools.partial(keygrad_kernel, scale),
        grid=(kv_heads,),
        in_specs=[
            score_block(tokens),
            score_block(tokens),
            score_block(pad),
            score_block(pad),
            row_block,
            row_block,
            score_block(1),
            pl.BlockSpec((rows, 1), lambda h: (0, 0)),
            row_block,
        ],
        out_specs=[
            pl.BlockSpec((2, tokens, 128), lambda h: (0, 0, h)),
            pl.BlockSpec((2, pad, 128), lambda h: (0, 0, h)),
            row_block,
        ],
        out_shape=[
            jax.ShapeDtypeStruct((2, tokens, kv_heads * 128), BF16),
            jax.ShapeDtypeStruct((2, pad, kv_heads * 128), BF16),
            jax.ShapeDtypeStruct(q.shape, BF16),
        ],
        compiler_params=pltpu.CompilerParams(vmem_limit_bytes=50 * 1024 * 1024),
        name="keygrad",
    )(e, g, er, gr, q, t, inv, row_grad, dq)


def shards(
    prompt_hidden,
    key_weight,
    value_weight,
    key_gain,
    queries,
    response_kv,
    targets,
    ref_scores,
    lengths,
    placement_map,
):
    hidden = prompt_hidden[0]
    prompt_rows, model_width = hidden.shape
    head_width = key_gain.shape[0]
    kv_width = key_weight.shape[1]
    kv_heads = kv_width // head_width
    resp_rows = queries.shape[1]
    query_heads = queries.shape[2] // head_width
    grouped = query_heads // kv_heads
    slot_count = lengths.shape[2]
    responses = ref_scores.shape[1]
    pair_count = responses // 2
    n_ctx = lax.axis_size("ctx")
    qk_scale = 1.0 / math.sqrt(head_width)

    hidden_columns = lax.all_to_all(
        hidden.reshape(prompt_rows, n_ctx, model_width // n_ctx).transpose(1, 0, 2),
        "ctx",
        split_axis=0,
        concat_axis=0,
        tiled=True,
    ).reshape(n_ctx * prompt_rows, model_width // n_ctx)

    raw_keys = jnp.dot(hidden, key_weight, preferred_element_type=F32).reshape(
        prompt_rows, kv_heads, head_width
    )
    inv_rms = lax.rsqrt(jnp.mean(raw_keys * raw_keys, axis=-1, keepdims=True) + NORM_EPS)
    prompt_keys = (raw_keys * inv_rms * key_gain).astype(BF16).reshape(prompt_rows, kv_width)
    prompt_values = jnp.dot(hidden, value_weight, preferred_element_type=F32).astype(BF16)
    gathered = lax.all_gather(
        jnp.stack([prompt_keys, prompt_values], axis=0), "ctx", axis=1, tiled=True
    )

    ends = jnp.cumsum(lengths[0, 0], dtype=jnp.int32)
    row_ids = lax.iota(jnp.int32, resp_rows)
    slot_ids = jnp.sum(
        (row_ids[:, None] >= ends[None, :]).astype(jnp.int32), axis=1, dtype=jnp.int32
    )
    same_slot = (slot_ids[:, None] == slot_ids[None, :]) & (row_ids[None, :] <= row_ids[:, None])
    slot_onehot = (slot_ids[:, None] == lax.iota(jnp.int32, slot_count)[None, :]).astype(F32)
    place_onehot = (placement_map[0][:, None] == lax.iota(jnp.int32, responses)[None, :]).astype(
        F32
    )
    pad = -resp_rows % 128
    bias = jnp.pad(
        jnp.where(same_slot, 0.0, MASK_FILL).astype(F32),
        ((0, 0), (0, pad)),
        constant_values=MASK_FILL,
    )
    resp = jnp.pad(response_kv[0], ((0, pad), (0, 0), (0, 0)))
    q, t = queries[0], targets[0]
    e, g, er, gr, inv, dq, token_part = attend(
        q, t, gathered[0], gathered[1], resp[:, 0], resp[:, 1], bias, qk_scale, grouped, 2
    )

    slot_part = jnp.sum(token_part * slot_onehot, axis=0)
    scores = lax.psum(
        jnp.sum(slot_part[:, None] * place_onehot, axis=0), ("ctx", "tp")
    )
    shifted = scores - ref_scores[0]
    margin = DPO_BETA * (shifted[:pair_count] - shifted[pair_count:])
    dpo_loss = jnp.sum(jax.nn.softplus(-margin))
    pair_grad = -DPO_BETA * jax.nn.sigmoid(-margin)
    score_grad = jnp.concatenate([pair_grad, -pair_grad])
    slot_grad = jnp.sum(place_onehot * score_grad[None, :], axis=1)
    row_grad = jnp.sum(slot_onehot * slot_grad[None, :], axis=1)

    dkv, drkv, query_grad = keygrad(e, g, er, gr, q, t, inv, row_grad[:, None], dq, qk_scale)
    response_kv_grad = jnp.stack([drkv[0, :resp_rows], drkv[1, :resp_rows]], axis=1)

    owned_grad = lax.psum_scatter(dkv, "ctx", scatter_dimension=1, tiled=True).astype(F32)
    gain_grad = key_gain * owned_grad[0].reshape(prompt_rows, kv_heads, head_width)
    raw_grad = inv_rms * gain_grad - raw_keys * inv_rms * inv_rms * inv_rms * jnp.mean(
        raw_keys * gain_grad, axis=-1, keepdims=True
    )
    kv_grad_b = jnp.stack([raw_grad.reshape(prompt_rows, kv_width), owned_grad[1]], axis=0).astype(
        BF16
    )
    gathered_grad = lax.all_gather(kv_grad_b, "ctx", axis=1, tiled=True)
    hidden_part = lax.dot_general(kv_grad_b[0], key_weight, NT, preferred_element_type=F32)
    hidden_part = hidden_part + lax.dot_general(
        kv_grad_b[1], value_weight, NT, preferred_element_type=F32
    )
    prompt_grad = lax.psum_scatter(
        hidden_part.astype(BF16), "tp", scatter_dimension=1, tiled=True
    )
    weight_part = jnp.stack(
        [
            lax.dot_general(hidden_columns, gathered_grad[0], TN, preferred_element_type=F32),
            lax.dot_general(hidden_columns, gathered_grad[1], TN, preferred_element_type=F32),
        ],
        axis=1,
    )
    weight_grad = lax.psum_scatter(weight_part, "dp", scatter_dimension=0, tiled=True)
    return (
        dpo_loss[None],
        query_grad[None],
        response_kv_grad[None],
        prompt_grad[None],
        weight_grad,
    )


def solution(mesh):
    in_specs = (
        P("dp", "ctx", None),
        P(None, "tp"),
        P(None, "tp"),
        P(),
        P("dp", "ctx", "tp"),
        P("dp", "ctx", None, "tp"),
        P("dp", "ctx", "tp"),
        P("dp", None),
        P("dp", "ctx", None),
        P("dp", "ctx"),
    )
    out_specs = (
        P("dp"),
        P("dp", "ctx", "tp"),
        P("dp", "ctx", None, "tp"),
        P("dp", "ctx", "tp"),
        P(("ctx", "dp"), None, "tp"),
    )
    return jax.shard_map(shards, mesh=mesh, in_specs=in_specs, out_specs=out_specs, check_vma=False)
```

time: 1360 us -> 448 us (0.33)
  waiting for transfers between devices: 1030 us -> 183 us
  matrix products: 117 us -> 17.5 us
  blocking collectives: 67.4 us -> 163 us
  local copies, waits for them, and re-layouts: 101 us -> 19.9 us
  Pallas kernels: 0 us -> 44.5 us
  other arithmetic: 25 us -> 5.05 us
    unnamed x5, waiting for transfers between devices: 890 us -> 0.08 us
    dot_general x39 -> x6, matrix products: 117 us -> 17.5 us  [the longest x1 5.05 us: shards(): lax.dot_general(kv_grad_b[1], value_weight, NT, preferred_element_type=F32)]
    psum x2 -> x1, blocking collectives: 67.4 us -> 138 us  [shards(): lax.psum(jnp.sum(slot_part[:, None] * place_onehot, axis=0), ('ctx', 'tp'))]
    pallas_call x0 -> x2, Pallas kernels: none -> 44.5 us  [the longest x1 30.1 us: attend(): pl.pallas_call(functools.partial(attend_kernel, scale), grid=(kv_heads, s...]
    all_gather x1 -> x2, waiting for transfers between devices: 44.2 us -> 75.5 us  [the longest x1 49.7 us: shards(): lax.all_gather(jnp.stack([prompt_keys, prompt_values], axis=0), 'ctx', ax...]
    reshape x1 -> x0, local copies, waits for them, and re-layouts: 30.9 us -> none  [shards(): product.reshape(model_width // lax.axis_size(('ctx', 'dp')) * lax.axis_si...]
    all_to_all x0 -> x1, blocking collectives: none -> 25.4 us  [shards(): lax.all_to_all(hidden.reshape(prompt_rows, n_ctx, model_width // n_ctx).t...]
    reduce_sum x7 -> x2, other arithmetic: 15.2 us -> 0.2 us  [the longest x1 0.12 us: shards(): slot_part = jnp.sum(token_part * slot_onehot, axis=0)]
  transfers between devices with their start and end apart: 4 -> 5, of which waited for: 4 -> 5; matrix products, arithmetic and copies ran while one was open for 2% -> 3% of each run, Pallas kernels for 0% -> 0%
where the time goes in v1:
time: 448 us; the launch traced here: 447 us
  waiting for transfers between devices  183 us (41%)
  blocking collectives  163 us (36%)
  Pallas kernels  44.5 us (10%)
  local copies, waits for them, and re-layouts  19.9 us (4%)
  matrix products  17.5 us (4%)
  between operations  14.1 us (3%)
  other arithmetic  5.05 us (1%)
    psum x1, blocking collectives, shards(): lax.psum(jnp.sum(slot_part[:, None] * place_onehot, axis=0), ('ctx', 'tp'))  138 us
    reduce_scatter x1, waiting for transfers between devices, shards(): lax.psum_scatter(dkv, 'ctx', scatter_dimension=1, tiled=True).astype(F32)  79.9 us
    all_gather x1, waiting for transfers between devices, shards(): lax.all_gather(jnp.stack([prompt_keys, prompt_values], axis=0), 'ctx', ax...  49.7 us
    pallas_call x1, Pallas kernels, attend(): pl.pallas_call(functools.partial(attend_kernel, scale), grid=(kv_heads, s...  30.1 us
    all_gather x1, waiting for transfers between devices, shards(): gathered_grad = lax.all_gather(kv_grad_b, 'ctx', axis=1, tiled=True)  25.9 us
    all_to_all x1, blocking collectives, shards(): lax.all_to_all(hidden.reshape(prompt_rows, n_ctx, model_width // n_ctx).t...  25.4 us
    reduce_scatter x1, waiting for transfers between devices, shards(): lax.psum_scatter(hidden_part.astype(BF16), 'tp', scatter_dimension=1, til...  18.8 us
    pallas_call x1, Pallas kernels, keygrad(): pl.pallas_call(functools.partial(keygrad_kernel, scale), grid=(kv_heads,)...  14.3 us
  transfers between devices with their start and end apart: 5, of which 5 were waited for; matrix products, arithmetic and copies ran while one was open for 3% of the time, Pallas kernels for 0%

profile of v1, /device:TPU:1, one launch (start us, length us, event | category | flops | bytes accessed | tf_op | source)
XLA Modules:
  0.0 447.2 jit_solution(9331121523070022511)
XLA Ops:
  7.2 7.9 %copy.65 = bf16[512,5120]{1,0:T(8,128)(2,1)} copy(bf16[512,5120]{0,1:T(8,128)(2,1)} %bitcast.79) | data formatting | bytes 10485760 | tf_op jit(solution)/shard_map/dot_general | solution.py:237
  15.1 3.6 fusion.5
  18.8 0.3 copy-done.3
  19.2 1.8 multiply_reduce_fusion.1
  21.0 0.6 copy-done.6
  21.8 0.7 pad_maximum_fusion.1
  22.6 0.2 reduce-window.8
  23.1 49.7 %all-gather.3.cloned.1.call-done = bf16[2,2048,512]{2,1,0:T(8,128)(2,1)} async-done(((bf16[2,64,512]{2,1,0:T(8,128)(2,1)}), bf16[2,2048,512]{2,1,0:T(8,128)(2,1)}) %all-gather.3.cloned.1.call-update) | async-done | bytes 4194320 | tf_op jit(solution)/shard_map/all_gather | solution.py:243
  72.7 4.5 slice_bitcast_fusion.4
  77.2 30.1 %attend.1 = (bf16[4,768,2048]{2,1,0:T(8,128)(2,1)}, bf16[4,768,2048]{2,1,0:T(8,128)(2,1)}, bf16[4,768,128]{2,1,0:T(8,128)(2,1)S(1)}, bf16[4,768,128]{2,1,0:T(8,1...) custom-call(bf16[96,4096]{1,0:T(8,128)(2,1)S(1)} %bitcast.75, ...), custom_call_target="tpu_custom_call" | custom-call | tf_op jit(solution)/shard_map/attend/pallas_call | solution.py:99
  107.3 0.9 copy-done.2
  108.5 138.1 %psum.7 = f32[256]{0:T(256)S(1)} all-reduce(f32[256]{0:T(256)S(1)} %select_reduce_fusion.1), channel_id=1, replica_groups=mesh['ctx'=32,'tp'=2,'dp'=2] {'ctx','tp'}, use_global_device_ids=true, to_apply=%region_5.6 | all-reduce | flops 256 | bytes 2048 | tf_op jit(solution)/shard_map/psum | solution.py:270
  246.6 0.2 select_reduce_fusion
  247.0 14.3 %keygrad.1 = (bf16[2,2048,512]{2,1,0:T(8,128)(2,1)}, bf16[2,128,512]{2,1,0:T(8,128)(2,1)S(1)}, bf16[96,4096]{1,0:T(8,128)(2,1)}) custom-call(bf16[4,768,2048]{2,1,0:T(8,128)(2,1)} %get-tuple-element.16.e_ref, bf16[4,768,2048]{2,1,0:T(8,128)(2,1)} %get-tuple-element.17.g_ref, bf16[4,768,128]{2,1,0:T(8,128)(2,1)S(1)} %get-tuple-element.18.er_ref, ...), custom_call_target="tpu_custom_call" | custom-call | tf_op jit(solution)/shard_map/keygrad/pallas_call | solution.py:174
  261.4 79.9 %reduce-scatter.4.cloned.1.call-done = bf16[2,64,512]{2,1,0:T(8,128)(2,1)} async-done(((bf16[2,2048,512]{2,1,0:T(8,128)(2,1)}), bf16[2,64,512]{2,1,0:T(8,128)(2,1)}) %reduce-scatter.4.cloned.1.call-update) | async-done | bytes 131088 | tf_op jit(solution)/shard_map/reduce_scatter | solution.py:284
  341.4 0.9 fusion.20
  342.7 0.7 pad_maximum_fusion.2
  343.4 1.3 reshape_squeeze.11
  344.7 0.6 copy.61
  345.3 25.4 %all_to_all.5 = bf16[32,64,160]{2,1,0:T(8,128)(2,1)S(1)} all-to-all(bf16[32,64,160]{2,1,0:T(8,128)(2,1)S(1)} %copy.61), channel_id=1, replica_groups=mesh['ctx'=32,'tp'=2,'dp'=2] {'ctx'}, dimensions={0} | all-to-all | bytes 1310720 | tf_op jit(solution)/shard_map/all_to_all | solution.py:229
  370.7 25.9 %all-gather.5.cloned.1.call-done = bf16[2,2048,512]{2,1,0:T(8,128)(2,1)} async-done(((bf16[2,64,512]{2,1,0:T(8,128)(2,1)}), bf16[2,2048,512]{2,1,0:T(8,128)(2,1)}) %all-gather.5.cloned.1.call-update) | async-done | bytes 4194320 | tf_op jit(solution)/shard_map/all_gather | solution.py:292
  396.6 2.3 fusion.4
  398.9 0.5 copy-done.13
  399.4 0.5 fusion.3
  400.0 0.9 pad_maximum_fusion
  400.9 4.2 fusion.11
  405.1 5.0 %fusion = bf16[64,5120]{1,0:T(8,128)(2,1)} fusion(f32[64,5120]{1,0:T(8,128)S(1)} %fusion.11, bf16[5120,512]{1,0:T(8,128)(2,1)} %param.12, bf16[2,64,512]{2,1,0:T(8,128)(2,1)S(1)} %copy-done.8), kind=kOutput, calls=%fused_computation.1 | convolution fusion | flops 336199680 | bytes 7274496 | tf_op jit(solution)/shard_map/dot_general | solution.py:294
  410.2 0.9 copy.63
  411.1 0.6 fusion.17
  411.7 8.2 %reduce-scatter.8.cloned.1.call-done = f32[80,2,512]{2,0,1:T(8,128)} async-done(((f32[160,2,512]{2,0,1:T(8,128)}), f32[80,2,512]{2,0,1:T(8,128)}) %reduce-scatter.8.cloned.1.call-update) | async-done | bytes 327696 | tf_op jit(solution)/shard_map/reduce_scatter | solution.py:307
  419.9 1.9 copy.64
  421.9 18.8 %reduce-scatter.6.cloned.1.call-done = bf16[64,2560]{1,0:T(8,128)(2,1)} async-done(((bf16[64,5120]{1,0:T(8,128)(2,1)}), bf16[64,2560]{1,0:T(8,128)(2,1)}) %reduce-scatter.6.cloned.1.call-update) | async-done | bytes 327696 | tf_op jit(solution)/shard_map/reduce_scatter | solution.py:297
  (61 shorter events, 1.7 us)
Async XLA Ops:
  7.2 65.5 %all-gather.3.cloned.1.call-start = ((), (), s32[]{:S(2)}) async-start(), calls=%async_computation.4 | async-start | bytes 4325376 | tf_op jit(solution)/shard_map/all_gather | solution.py:243
  7.2 7.9 %copy-start.4 = (bf16[1,64,5120]{2,1,0:T(8,128)(2,1)S(1)}, bf16[1,64,5120]{2,1,0:T(8,128)(2,1)}, u32[]{:S(2)}) copy-start(bf16[1,64,5120]{2,1,0:T(8,128)(2,1)} %param.10) | copy-start | bytes 1966084
  15.1 4.0 copy-start.3
  18.8 2.9 copy-start.10
  18.8 3.8 copy-start.9
  18.8 3.8 copy-start.14
  21.0 0.7 copy-start.6
  22.5 318.8 %reduce-scatter.4.cloned.1.call-start = ((), (), s32[]{:S(2)}) async-start(), calls=%async_computation.5 | async-start | bytes 4325376 | tf_op jit(solution)/shard_map/reduce_scatter | solution.py:284
  23.0 54.1 %copy-start = (bf16[1,96,4096]{2,1,0:T(8,128)(2,1)S(1)}, bf16[1,96,4096]{2,1,0:T(8,128)(2,1)}, u32[]{:S(2)}) copy-start(bf16[1,96,4096]{2,1,0:T(8,128)(2,1)} %param.14) | copy-start | bytes 2359300
  77.2 31.3 %copy-start.11 = (s32[1,8]{1,0:T(1,128)S(1)}, s32[1,8]{1,0:T(1,128)}, u32[]{:S(2)}) copy-start(s32[1,8]{1,0:T(1,128)} %param.19) | copy-start | bytes 100
  77.2 169.4 %copy-start.12 = (f32[1,256]{1,0:T(1,128)S(1)}, f32[1,256]{1,0:T(1,128)}, u32[]{:S(2)}) copy-start(f32[1,256]{1,0:T(1,128)} %param.17) | copy-start | bytes 3076
  77.2 169.9 %copy-start.1 = (bf16[1,96,4096]{2,1,0:T(8,128)(2,1)S(1)}, bf16[1,96,4096]{2,1,0:T(8,128)(2,1)}, u32[]{:S(2)}) copy-start(bf16[1,96,4096]{2,1,0:T(8,128)(2,1)} %param.16) | copy-start | bytes 2359300
  107.3 0.9 copy-start.2
  261.3 81.0 %copy-start.7 = (f32[64,4,128]{2,0,1:T(8,128)S(1)}, f32[64,4,128]{2,0,1:T(8,128)}, u32[]{:S(2)}) copy-start(f32[64,4,128]{2,0,1:T(8,128)} %copy-done.6) | copy-start | bytes 393220
  261.4 82.1 %copy-start.5 = (bf16[1,64,5120]{2,1,0:T(8,128)(2,1)S(1)}, bf16[1,64,5120]{2,1,0:T(8,128)(2,1)}, u32[]{:S(2)}) copy-start(bf16[1,64,5120]{2,1,0:T(8,128)(2,1)} %param.10) | copy-start | bytes 1966084
  261.4 135.2 %all-gather.5.cloned.1.call-start = ((), (), s32[]{:S(2)}) async-start(), calls=%async_computation.7 | async-start | bytes 4325376 | tf_op jit(solution)/shard_map/all_gather | solution.py:292
  343.4 76.6 %reduce-scatter.8.cloned.1.call-start = ((), (), s32[]{:S(2)}) async-start(), calls=%async_computation.8 | async-start | bytes 983040 | tf_op jit(solution)/shard_map/reduce_scatter | solution.py:307
  396.6 2.8 copy-start.13
  399.9 5.1 %copy-start.8 = (bf16[2,64,512]{2,1,0:T(8,128)(2,1)S(1)}, bf16[2,64,512]{2,1,0:T(8,128)(2,1)}, u32[]{:S(2)}) copy-start(bf16[2,64,512]{2,1,0:T(8,128)(2,1)} %reduce-scatter.4.cloned.1.call-done) | copy-start | bytes 393220
  400.9 39.8 %reduce-scatter.6.cloned.1.call-start = ((), (), s32[]{:S(2)}) async-start(), calls=%async_computation.6 | async-start | bytes 983040 | tf_op jit(solution)/shard_map/reduce_scatter | solution.py:297
Sparse Core Ops, SparseCore 0:
  22.7 50.0 all-gather.2
  261.5 79.8 reduce-scatter.3
  344.6 51.9 all-gather.4
  401.0 18.9 reduce-scatter.7
  422.7 17.9 reduce-scatter.5

commit v2 on v1

v2 whole, which is shorter than its diff:
```python
import functools
import math

import jax
import jax.numpy as jnp
from jax import lax
from jax.experimental import pallas as pl
from jax.experimental.pallas import tpu as pltpu
from jax.sharding import PartitionSpec as P

NORM_EPS = 1e-06
DPO_BETA = 0.5
MASK_FILL = -1e30
LOG2E = 1.4426950408889634
NT = (((1,), (1,)), ((), ()))
TN = (((0,), (0,)), ((), ()))
F32 = jnp.float32
BF16 = jnp.bfloat16


MESH = pl.DeviceIdType.MESH
SIDE = 4


def params(limit_mib, **more):
    return pltpu.CompilerParams(vmem_limit_bytes=limit_mib * 1024 * 1024, **more)


def place():
    me = lax.axis_index("ctx")
    return me // (2 * SIDE), (me // 2) % SIDE, me % 2


def ctx_id(x, z, core):
    return {"ctx": (x * SIDE + z) * 2 + core}


def greet(peers):
    barrier = pltpu.get_barrier_semaphore()
    for peer in peers:
        pl.semaphore_signal(barrier, inc=1, device_id=peer, device_id_type=MESH)
    pl.semaphore_wait(barrier, len(peers))


def plane_peers():
    x, z, core = place()
    return [
        ctx_id((x + 1) % SIDE, z, core),
        ctx_id((x + SIDE - 1) % SIDE, z, core),
        ctx_id(x, (z + 1) % SIDE, core),
        ctx_id(x, (z + SIDE - 1) % SIDE, core),
        ctx_id(x, z, 1 - core),
    ]


def ring(axis):
    x, z, core = place()
    if axis == 0:
        return x, lambda p: ctx_id(p, z, core)
    return z, lambda p: ctx_id(x, p, core)


def around(p):
    return (p + 1) % SIDE, (p + SIDE - 1) % SIDE, (p + 2) % SIDE


class Copies:
    def __init__(self, send_sem, recv_sem):
        self.send_sem, self.recv_sem, self.started = send_sem, recv_sem, []

    def make(self, src, dst, peer, slot):
        return pltpu.make_async_remote_copy(
            src_ref=src,
            dst_ref=dst,
            send_sem=self.send_sem.at[slot],
            recv_sem=self.recv_sem.at[slot],
            device_id=peer,
            device_id_type=MESH,
        )

    def send(self, src, dst, peer, slot):
        one = self.make(src, dst, peer, slot)
        one.start()
        self.started.append(one)

    def arrived(self, dst, slot):
        x, z, core = place()
        self.make(dst, dst, ctx_id(x, z, 1 - core), slot).wait_recv()

    def finish(self):
        for one in self.started:
            one.wait_send()


GATHER_COPIES = 72


def gather_stages(refs, copies):
    x, z, core = place()
    partner = ctx_id(x, z, 1 - core)
    rows = refs[0].shape[3]
    full, low, high = pl.ds(0, rows), pl.ds(0, rows // 2), pl.ds(rows // 2, rows // 2)
    rings = {}
    for kv in range(2):
        for level in range(2):
            p, at = ring(kv if level == 0 else 1 - kv)
            right, left, opposite = around(p)
            rings[kv, level] = ((p, left, right, opposite), at(right), at(left))

    def block(kv, i, j, part=full, of_core=None):
        of_core = core if of_core is None else of_core
        i, j = rings[kv, 0][0][i], rings[kv, 1][0][j]
        spot = (i, j) if kv == 0 else (j, i)
        return refs[kv].at[spot[0], spot[1], of_core, part]

    def first(kv, k):
        return kv * 36 + k

    def second(kv, i, k):
        return kv * 36 + 4 + i * 4 + k

    def swap_slot(kv, i, j):
        return kv * 36 + 20 + i * 4 + j

    def send(ref, peer, slot):
        copies.send(ref, ref, peer, slot)

    def to_core(kv, i, j):
        send(block(kv, i, j), partner, swap_slot(kv, i, j))

    def onward(kv, i):
        _, right, left = rings[kv, 1]
        send(block(kv, i, 0), right, second(kv, i, 0))
        send(block(kv, i, 0), left, second(kv, i, 1))
        to_core(kv, i, 0)

    def open_all():
        for kv in range(2):
            _, right, left = rings[kv, 0]
            send(block(kv, 0, 0), right, first(kv, 0))
            send(block(kv, 0, 0), left, first(kv, 1))
        for kv in range(2):
            onward(kv, 0)

    def first_neighbours():
        for kv in range(2):
            _, right, left = rings[kv, 0]
            copies.arrived(block(kv, 1, 0), first(kv, 0))
            send(block(kv, 1, 0, low), right, first(kv, 2))
            onward(kv, 1)
            copies.arrived(block(kv, 2, 0), first(kv, 1))
            send(block(kv, 2, 0, high), left, first(kv, 3))
            onward(kv, 2)

    def first_opposite():
        for kv in range(2):
            copies.arrived(block(kv, 3, 0, low), first(kv, 2))
            copies.arrived(block(kv, 3, 0, high), first(kv, 3))
            onward(kv, 3)

    def second_neighbours(i):
        for kv in range(2):
            _, right, left = rings[kv, 1]
            copies.arrived(block(kv, i, 1), second(kv, i, 0))
            send(block(kv, i, 1, low), right, second(kv, i, 2))
            to_core(kv, i, 1)
            copies.arrived(block(kv, i, 2), second(kv, i, 1))
            send(block(kv, i, 2, high), left, second(kv, i, 3))
            to_core(kv, i, 2)

    def second_opposite(i):
        for kv in range(2):
            copies.arrived(block(kv, i, 3, low), second(kv, i, 2))
            copies.arrived(block(kv, i, 3, high), second(kv, i, 3))
            to_core(kv, i, 3)

    def from_core(kv):
        for i in range(4):
            for j in range(4):
                copies.arrived(block(kv, i, j, full, 1 - core), swap_slot(kv, i, j))

    return [
        open_all,
        first_neighbours,
        lambda: second_neighbours(0),
        first_opposite,
        lambda: second_neighbours(1),
        lambda: second_opposite(0),
        lambda: second_neighbours(2),
        lambda: second_opposite(1),
        lambda: second_neighbours(3),
        lambda: second_opposite(2),
        lambda: second_opposite(3),
        lambda: from_core(0),
        lambda: from_core(1),
    ]


def project_kernel(
    h_ref,
    kw_ref,
    vw_ref,
    gain_ref,
    raw_ref,
    gk_ref,
    gv_ref,
    w_ref,
    load_sem,
    send_sem,
    recv_sem,
):
    x, z, core = place()
    steps, tile, width = w_ref.shape[1:]

    def load(kv, i):
        src = (kw_ref, vw_ref)[kv].at[pl.ds(i * tile, tile)]
        return pltpu.make_async_copy(src, w_ref.at[kv, i], load_sem.at[kv, i])

    for i in range(steps):
        for kv in range(2):
            load(kv, i).start()
    greet(plane_peers())
    sums = [jnp.zeros((h_ref.shape[0], width), F32)] * 2
    for i in range(steps):
        part = h_ref[:, i * tile : (i + 1) * tile]
        for kv in range(2):
            load(kv, i).wait()
            sums[kv] = sums[kv] + jnp.dot(part, w_ref[kv, i], preferred_element_type=F32)
    raw_ref[...] = sums[0]
    gv_ref[x, z, core] = sums[1].astype(BF16)
    parts = []
    for i in range(width // 128):
        keys = sums[0][:, i * 128 : (i + 1) * 128]
        inv = lax.rsqrt(jnp.mean(keys * keys, axis=1, keepdims=True) + NORM_EPS)
        parts.append((keys * inv * gain_ref[...]).astype(BF16))
    gk_ref[x, z, core] = jnp.concatenate(parts, axis=1)
    copies = Copies(send_sem, recv_sem)
    for stage in gather_stages((gk_ref, gv_ref), copies):
        stage()
    copies.finish()


def project_and_gather(hidden, key_weight, value_weight, gain):
    rows, depth = hidden.shape
    width = key_weight.shape[1]
    tile = 1024
    steps = depth // tile
    vmem, anywhere = pl.BlockSpec(memory_space=pltpu.VMEM), pl.BlockSpec(memory_space=pl.ANY)
    plane = jax.ShapeDtypeStruct((SIDE, SIDE, 2, rows, width), BF16)
    raw, keys, values = pl.pallas_call(
        project_kernel,
        out_shape=[jax.ShapeDtypeStruct((rows, width), F32), plane, plane],
        in_specs=[vmem, anywhere, anywhere, vmem],
        out_specs=[vmem] * 3,
        scratch_shapes=[
            pltpu.VMEM((2, steps, tile, width), BF16),
            pltpu.SemaphoreType.DMA((2, steps)),
            pltpu.SemaphoreType.DMA((GATHER_COPIES,)),
            pltpu.SemaphoreType.DMA((GATHER_COPIES,)),
        ],
        compiler_params=params(60, collective_id=0, has_side_effects=True),
        name="project_and_gather",
    )(hidden, key_weight, value_weight, gain)
    total = SIDE * SIDE * 2 * rows
    return raw, keys.reshape(total, width), values.reshape(total, width)


def attend_kernel(
    scale,
    q_ref,
    t_ref,
    k_ref,
    v_ref,
    rk_ref,
    rv_ref,
    bias_ref,
    h_ref,
    e_ref,
    g_ref,
    inv_ref,
    dq_ref,
    tok_ref,
    o_ref,
    own_sem,
    send_sem,
    recv_sem,
):
    me = lax.axis_index("ctx")
    n = o_ref.shape[0]

    def window(peer):
        tile = 5 * (peer // 4) + peer % 4
        return h_ref.at[:, pl.ds(pl.multiple_of(tile * 128, 128), WINDOW)]

    def copy(k):
        peer = (me + k) % n
        return pltpu.make_async_remote_copy(
            src_ref=window(peer),
            dst_ref=o_ref.at[me],
            send_sem=send_sem.at[k - 1],
            recv_sem=recv_sem.at[k - 1],
            device_id={"ctx": peer},
            device_id_type=MESH,
        )

    own_copy = pltpu.make_async_copy(window(me), o_ref.at[me], own_sem)

    @pl.when((pl.program_id(0) == 0) & (pl.program_id(1) == 0))
    def _():
        barrier = pltpu.get_barrier_semaphore()

        def hello(k, carry):
            pl.semaphore_signal(
                barrier, inc=1, device_id={"ctx": (me + k) % n}, device_id_type=MESH
            )
            return carry

        def go(k, carry):
            copy(k).start()
            return carry

        lax.fori_loop(1, n, hello, 0)
        pl.semaphore_wait(barrier, n - 1)
        lax.fori_loop(1, n, go, 0)
        own_copy.start()

    heads = q_ref.shape[1] // 128
    rows = q_ref.shape[0]
    q = jnp.concatenate([q_ref[:, i * 128 : (i + 1) * 128] for i in range(heads)], axis=0)
    t = jnp.concatenate([t_ref[:, i * 128 : (i + 1) * 128] for i in range(heads)], axis=0)
    bias = jnp.concatenate([bias_ref[...]] * heads, axis=0)
    k, v, rk, rv = k_ref[...], v_ref[...], rk_ref[...], rv_ref[...]
    s = lax.dot_general(q, k, NT, preferred_element_type=F32)
    sr = lax.dot_general(q, rk, NT, preferred_element_type=F32) + bias
    peak = jnp.maximum(
        jnp.max(s, axis=1, keepdims=True), jnp.max(sr, axis=1, keepdims=True)
    )
    factor = scale * LOG2E
    top = peak * factor
    e = jnp.exp2(s * factor - top)
    er = jnp.exp2(sr * factor - top)
    inv = 1.0 / (jnp.sum(e, axis=1, keepdims=True) + jnp.sum(er, axis=1, keepdims=True))
    eb, erb = e.astype(BF16), er.astype(BF16)
    tokens = k.shape[0]
    e_ref[0, :, :tokens] = eb
    e_ref[0, :, tokens:] = erb
    attended = (
        jnp.dot(eb, v, preferred_element_type=F32) + jnp.dot(erb, rv, preferred_element_type=F32)
    ) * inv
    dot = jnp.sum(attended * t.astype(F32), axis=1, keepdims=True)
    dp = lax.dot_general(t, v, NT, preferred_element_type=F32)
    dpr = lax.dot_general(t, rv, NT, preferred_element_type=F32)
    gb = (eb.astype(F32) * (dp - dot)).astype(BF16)
    grb = (erb.astype(F32) * (dpr - dot)).astype(BF16)
    g_ref[0, :, :tokens] = gb
    g_ref[0, :, tokens:] = grb
    dq = (
        jnp.dot(gb, k, preferred_element_type=F32) + jnp.dot(grb, rk, preferred_element_type=F32)
    ) * (inv * scale)
    inv_ref[0] = inv
    for i in range(heads):
        dq_ref[:, i * 128 : (i + 1) * 128] = dq[i * rows : (i + 1) * rows].astype(BF16)

    @pl.when((pl.program_id(0) == 0) & (pl.program_id(1) == 0))
    def _():
        tok_ref[...] = jnp.zeros_like(tok_ref)

    total = dot[:rows]
    for i in range(1, heads):
        total = total + dot[i * rows : (i + 1) * rows]
    tok_ref[...] += total

    @pl.when(
        (pl.program_id(0) == pl.num_programs(0) - 1) & (pl.program_id(1) == pl.num_programs(1) - 1)
    )
    def _():
        def done(k, carry):
            copy(k).wait()
            return carry

        own_copy.wait()
        lax.fori_loop(1, n, done, 0)


WINDOW = 256


def attend(q, t, prompt_keys, prompt_values, rk, rv, bias, hidden, n, scale, grouped, chunk):
    rows = q.shape[0]
    tokens, kv_width = prompt_keys.shape
    kv_heads = kv_width // 128
    pad = rk.shape[0]
    steps = grouped // chunk
    m = chunk * rows
    total = grouped * rows
    row_block = pl.BlockSpec((rows, chunk * 128), lambda h, c: (0, h * steps + c))
    head_block = pl.BlockSpec((tokens, 128), lambda h, c: (0, h))
    resp_block = pl.BlockSpec((pad, 128), lambda h, c: (0, h))

    def score_block(width):
        return pl.BlockSpec((1, m, width), lambda h, c: (h, c, 0))

    return pl.pallas_call(
        functools.partial(attend_kernel, scale),
        grid=(kv_heads, steps),
        in_specs=[
            row_block,
            row_block,
            head_block,
            head_block,
            resp_block,
            resp_block,
            pl.BlockSpec((rows, pad), lambda h, c: (0, 0)),
            pl.BlockSpec(memory_space=pl.ANY),
        ],
        out_specs=[
            score_block(tokens + pad),
            score_block(tokens + pad),
            score_block(1),
            row_block,
            pl.BlockSpec((rows, 1), lambda h, c: (0, 0)),
            pl.BlockSpec(memory_space=pl.ANY),
        ],
        out_shape=[
            jax.ShapeDtypeStruct((kv_heads, total, tokens + pad), BF16),
            jax.ShapeDtypeStruct((kv_heads, total, tokens + pad), BF16),
            jax.ShapeDtypeStruct((kv_heads, total, 1), F32),
            jax.ShapeDtypeStruct(q.shape, BF16),
            jax.ShapeDtypeStruct((rows, 1), F32),
            jax.ShapeDtypeStruct((n, hidden.shape[0], WINDOW), BF16),
        ],
        scratch_shapes=[
            pltpu.SemaphoreType.DMA,
            pltpu.SemaphoreType.DMA((n - 1,)),
            pltpu.SemaphoreType.DMA((n - 1,)),
        ],
        compiler_params=params(56, collective_id=3, has_side_effects=True),
        name="attend",
    )(q, t, prompt_keys, prompt_values, rk, rv, bias, hidden)


def norm_backward(raw, gain, grad):
    parts = []
    for h in range(raw.shape[1] // 128):
        keys = raw[:, h * 128 : (h + 1) * 128]
        kg = gain * grad[:, h * 128 : (h + 1) * 128]
        inv = lax.rsqrt(jnp.mean(keys * keys, axis=1, keepdims=True) + NORM_EPS)
        mix = jnp.mean(keys * kg, axis=1, keepdims=True)
        parts.append(inv * kg - keys * (inv * inv * inv) * mix)
    return jnp.concatenate(parts, axis=1)


def total_of(*refs):
    value = refs[0][...].astype(F32)
    for ref in refs[1:]:
        value = value + ref[...].astype(F32)
    return value


REDUCE_COPIES = 68


class Reduce:
    def __init__(self, d_ref, c_ref, a_ref, b_ref, r_ref, s_ref, copies):
        self.d, self.c, self.a, self.b, self.r, self.s = d_ref, c_ref, a_ref, b_ref, r_ref, s_ref
        self.copies = copies
        x, z, self.core = place()
        self.partner = ctx_id(x, z, 1 - self.core)
        rows = a_ref.shape[3]
        self.low, self.high = pl.ds(0, rows // 2), pl.ds(rows // 2, rows // 2)
        self.rings = {}
        for kv in range(2):
            for inner in range(2):
                p, at = ring(1 - kv if inner else kv)
                right, left, opposite = around(p)
                self.rings[kv, inner] = ((opposite, right, left, p), at(right), at(left))

    def place_of(self, kv, i):
        return self.rings[kv, 0][0][i]

    def to_core(self, kv, i):
        self.copies.send(
            self.d.at[kv, i, :, 1 - self.core], self.c.at[kv, i], self.partner, kv * 4 + i
        )

    def landing(self, kv, i, k):
        return self.s.at[kv, k] if i is None else self.b.at[kv, i, k]

    def slot(self, kv, i, k):
        return 56 + kv * 6 + k if i is None else 8 + (kv * 4 + i) * 6 + k

    def unit(self, kv, i, j, part):
        if i is None:
            return self.r.at[kv, j, part]
        return self.a.at[kv, i, self.rings[kv, 1][0][j], part]

    def message(self, kv, i, k, ref):
        _, right, left = self.rings[kv, 0 if i is None else 1]
        peer = right if k in (0, 2, 4) else left
        self.copies.send(ref, self.landing(kv, i, k), peer, self.slot(kv, i, k))

    def landed(self, kv, i, k):
        ref = self.landing(kv, i, k)
        self.copies.arrived(ref, self.slot(kv, i, k))
        return ref

    def opening(self, kv, i, j):
        if j == 0:
            self.message(kv, i, 0, self.unit(kv, i, 0, self.low))
            self.message(kv, i, 1, self.unit(kv, i, 0, self.high))
        if j == 1:
            self.message(kv, i, 2, self.unit(kv, i, 1, self.high))
        if j == 2:
            self.message(kv, i, 3, self.unit(kv, i, 2, self.low))

    def passing(self, kv, i):
        for k, j, part in ((0, 1, self.low), (1, 2, self.high)):
            came = self.landed(kv, i, k)
            mine = self.unit(kv, i, j, part)
            mine[...] = total_of(mine, came).astype(BF16)
            self.message(kv, i, 4 + k, mine)

    def result(self, kv, i):
        lows = total_of(
            self.unit(kv, i, 3, self.low), self.landed(kv, i, 3), self.landed(kv, i, 4)
        )
        highs = total_of(
            self.unit(kv, i, 3, self.high), self.landed(kv, i, 2), self.landed(kv, i, 5)
        )
        return jnp.concatenate([lows, highs], axis=0)

    def start_inner(self, kv, i):
        self.copies.arrived(self.c.at[kv, i], kv * 4 + i)
        self.a[kv, i] = total_of(self.d.at[kv, i, :, self.core], self.c.at[kv, i]).astype(BF16)
        for j in range(3):
            self.opening(kv, i, j)

    def end_inner(self, kv, i):
        self.r[kv, i] = self.result(kv, i).astype(BF16)
        self.opening(kv, None, i)


def share_scores(buf, me, peer, copies, base):
    sent = []
    for k in range(1, 8):
        copies.send(buf.at[me], buf.at[me], peer(k), base + k - 1)
    for k in range(1, 8):
        copies.arrived(buf.at[(me - k + 8) % 8], base + k - 1)
    value = buf[0]
    for i in range(1, 8):
        value = value + buf[i]
    return value


def backward_kernel(
    scale,
    token_ref,
    pick_ref,
    ref_ref,
    q_ref,
    t_ref,
    inv_ref,
    raw_ref,
    gain_ref,
    e_ref,
    g_ref,
    kw_ref,
    vw_ref,
    hw_ref,
    loss_ref,
    row_ref,
    resp_ref,
    pgrad_ref,
    wgrad_ref,
    one_ref,
    two_ref,
    qs_ref,
    ts_ref,
    gbuf_ref,
    ebuf_ref,
    rbuf_ref,
    d_ref,
    c_ref,
    a_ref,
    b_ref,
    r_ref,
    s_ref,
    gk_ref,
    gv_ref,
    w_ref,
    h_ref,
    paway_ref,
    pcame_ref,
    pown_ref,
    wpart_ref,
    waway_ref,
    wcame_ref,
    load_sem,
    score_send,
    score_recv,
    reduce_send,
    reduce_recv,
    gather_send,
    gather_recv,
    last_send,
    last_recv,
):
    x, z, core = place()
    ctx, tp, dp = lax.axis_index("ctx"), lax.axis_index("tp"), lax.axis_index("dp")
    kv_heads, total, _ = qs_ref.shape
    rows = q_ref.shape[0]
    grouped = total // rows
    tokens = e_ref.shape[2] - rbuf_ref.shape[3]
    chunk = gbuf_ref.shape[3]
    unit = chunk // SIDE

    reduce_copies = Copies(reduce_send, reduce_recv)
    reduce = Reduce(d_ref, c_ref, a_ref, b_ref, r_ref, s_ref, reduce_copies)

    def loads(i):
        buf = i % 2
        start = pl.multiple_of(reduce.place_of(0, i) * chunk, chunk)
        parts = [
            pltpu.make_async_copy(
                g_ref.at[:, :, pl.ds(start, chunk)], gbuf_ref.at[buf], load_sem.at[buf, 0]
            )
        ]
        for j in range(SIDE):
            start = pl.multiple_of(j * chunk + reduce.place_of(1, i) * unit, unit)
            parts.append(
                pltpu.make_async_copy(
                    e_ref.at[:, :, pl.ds(start, unit)],
                    ebuf_ref.at[buf, :, :, pl.ds(j * unit, unit)],
                    load_sem.at[buf, 1 + j],
                )
            )
        return parts

    def start(parts):
        for one in parts:
            one.start()

    def wait(parts):
        for one in parts:
            one.wait()

    tail = pl.ds(tokens, rbuf_ref.shape[3])
    more = [
        pltpu.make_async_copy(g_ref.at[:, :, tail], rbuf_ref.at[0], load_sem.at[2, 0]),
        pltpu.make_async_copy(e_ref.at[:, :, tail], rbuf_ref.at[1], load_sem.at[2, 1]),
    ]
    late = [
        pltpu.make_async_copy(kw_ref, w_ref.at[0], load_sem.at[2, 2]),
        pltpu.make_async_copy(vw_ref, w_ref.at[1], load_sem.at[2, 3]),
        pltpu.make_async_copy(hw_ref, h_ref, load_sem.at[2, 4]),
    ]
    for i in range(2):
        start(loads(i))

    def first(k):
        q = (x * 2 + tp + k) % 8
        return {"ctx": ((q // 2) * SIDE + z) * 2 + core, "tp": q % 2}

    def second(k):
        q = (z * 2 + core + k) % 8
        return {"ctx": x * SIDE * 2 + q}

    other_dp = {"dp": 1 - dp}
    greet([first(k) for k in range(1, 8)] + [second(k) for k in range(1, 8)] + [other_dp])
    score_copies = Copies(score_send, score_recv)
    pick = pick_ref[...]
    part = jnp.sum(pick * token_ref[...], axis=0, keepdims=True)
    one_ref[x * 2 + tp] = jnp.broadcast_to(part, one_ref.shape[1:])
    half_sum = share_scores(one_ref, x * 2 + tp, first, score_copies, 0)
    two_ref[z * 2 + core] = half_sum
    scores = share_scores(two_ref, z * 2 + core, second, score_copies, 7)[:1]
    pairs = scores.shape[1] // 2
    shifted = scores - ref_ref[...]
    margin = DPO_BETA * (shifted[:, :pairs] - shifted[:, pairs:])
    small = jnp.exp(-jnp.abs(margin))
    pair_grad = -DPO_BETA * jnp.where(margin >= 0.0, small, 1.0) / (1.0 + small)
    score_grad = jnp.concatenate([pair_grad, -pair_grad], axis=1)
    row_grad = jnp.sum(pick * score_grad, axis=1, keepdims=True)
    row_ref[...] = row_grad
    row_factor = jnp.concatenate([row_grad] * grouped, axis=0)
    start(more)
    for h in range(kv_heads):
        factor = inv_ref[h] * row_factor
        base = h * grouped * 128
        pieces = [q_ref[:, base + i * 128 : base + (i + 1) * 128] for i in range(grouped)]
        q = jnp.concatenate(pieces, axis=0).astype(F32)
        qs_ref[h] = (q * (factor * scale)).astype(BF16)
        pieces = [t_ref[:, base + i * 128 : base + (i + 1) * 128] for i in range(grouped)]
        t = jnp.concatenate(pieces, axis=0).astype(F32)
        ts_ref[h] = (t * factor).astype(BF16)

    def chunk_grads(i):
        buf = i % 2
        for kv, (kept, scaled) in enumerate(((gbuf_ref, qs_ref), (ebuf_ref, ts_ref))):
            for h in range(kv_heads):
                grads = lax.dot_general(kept[buf, h], scaled[h], TN, preferred_element_type=F32)
                grads = grads.astype(BF16).reshape(SIDE, 2, unit // 2, 128)
                d_ref[kv, i, :, :, :, h * 128 : (h + 1) * 128] = grads
            reduce.to_core(kv, i)

    for i in range(SIDE):
        wait(loads(i))
        chunk_grads(i)
        if i + 2 < SIDE:
            start(loads(i + 2))
        if i == SIDE - 2:
            start(late)
        if i >= 1:
            for kv in range(2):
                reduce.start_inner(kv, i - 1)
        if i >= 2:
            for kv in range(2):
                reduce.passing(kv, i - 2)
        if i >= 3:
            for kv in range(2):
                reduce.end_inner(kv, i - 3)
    for kv in range(2):
        reduce.start_inner(kv, 3)
    for kv in range(2):
        reduce.passing(kv, 2)
    for kv in range(2):
        reduce.end_inner(kv, 1)
    for kv in range(2):
        reduce.passing(kv, 3)
    wait(more)
    for kv, scaled in enumerate((qs_ref, ts_ref)):
        for h in range(kv_heads):
            grads = lax.dot_general(rbuf_ref[kv, h], scaled[h], TN, preferred_element_type=F32)
            resp_ref[kv, :, h * 128 : (h + 1) * 128] = grads[:rows].astype(BF16)
    loss = jnp.maximum(-margin, 0.0) + jnp.log1p(small)
    loss_ref[...] = jnp.sum(loss, axis=1, keepdims=True)
    for kv in range(2):
        reduce.end_inner(kv, 2)
    for kv in range(2):
        reduce.passing(kv, None)
    for kv in range(2):
        reduce.end_inner(kv, 3)
    key_sum = reduce.result(0, None)
    gk_ref[x, z, core] = norm_backward(raw_ref[...], gain_ref[...], key_sum).astype(BF16)
    gv_ref[x, z, core] = reduce.result(1, None).astype(BF16)

    gather_copies = Copies(gather_send, gather_recv)
    stages = gather_stages((gk_ref, gv_ref), gather_copies)
    last_copies = Copies(last_send, last_recv)
    stages[0]()
    wait(late)
    tile = 512
    half = paway_ref.shape[1]

    def input_grad(side, store):
        key_grad, value_grad = gk_ref[x, z, core], gv_ref[x, z, core]

        def step(i, carry):
            here = pl.ds(pl.multiple_of(side * half + i * tile, tile), tile)
            value = lax.dot_general(key_grad, w_ref[0, here], NT, preferred_element_type=F32)
            value += lax.dot_general(value_grad, w_ref[1, here], NT, preferred_element_type=F32)
            store(pl.ds(pl.multiple_of(i * tile, tile), tile), value)
            return carry

        lax.fori_loop(0, half // tile, step, 0)

    def store_away(here, value):
        paway_ref[:, here] = value.astype(BF16)

    def store_own(here, value):
        pown_ref[:, here] = value

    input_grad(1 - tp, store_away)
    last_copies.send(paway_ref, pcame_ref, {"tp": 1 - tp}, 0)
    for stage in stages[1:5]:
        stage()
    input_grad(tp, store_own)
    for stage in stages[5:-2]:
        stage()
    last_copies.arrived(pcame_ref, 0)
    pgrad_ref[...] = (pown_ref[...] + pcame_ref[...].astype(F32)).astype(BF16)

    out_rows = wgrad_ref.shape[1]
    shift = (ctx % 4) * 32
    hidden = h_ref[...].reshape(-1, h_ref.shape[2])
    for kv, ref in enumerate((gk_ref, gv_ref)):
        stages[-2 + kv]()
        grads = ref[...].reshape(-1, ref.shape[4])
        wpart_ref[kv] = lax.dot_general(hidden, grads, TN, preferred_element_type=F32)
        away = pl.ds(pl.multiple_of(shift + (1 - dp) * out_rows, 16), out_rows)
        waway_ref[kv] = wpart_ref[kv, away].astype(BF16)
        last_copies.send(waway_ref.at[kv], wcame_ref.at[kv], other_dp, 1 + kv)
    for copies in (score_copies, reduce_copies, gather_copies):
        copies.finish()
    own = pl.ds(pl.multiple_of(shift + dp * out_rows, 16), out_rows)
    for kv in range(2):
        last_copies.arrived(wcame_ref.at[kv], 1 + kv)
        wgrad_ref[kv] = wpart_ref[kv, own] + wcame_ref[kv].astype(F32)
    last_copies.finish()


def backward(
    token_part, pick, ref_scores, q, t, inv, raw_keys, gain, e, g, kw, vw, windows, scale, out_rows
):
    rows, responses = pick.shape
    kv_heads, total, width = e.shape
    prompt_rows, kv_width = raw_keys.shape
    depth = kw.shape[0]
    n = windows.shape[0]
    tokens = n * prompt_rows
    pad = width - tokens
    chunk = tokens // SIDE
    half = depth // 2
    vmem, anywhere = pl.BlockSpec(memory_space=pltpu.VMEM), pl.BlockSpec(memory_space=pl.ANY)
    dma = pltpu.SemaphoreType.DMA
    small = (prompt_rows // 2, kv_width)
    return pl.pallas_call(
        functools.partial(backward_kernel, scale),
        out_shape=[
            jax.ShapeDtypeStruct((1, 1), F32),
            jax.ShapeDtypeStruct((rows, 1), F32),
            jax.ShapeDtypeStruct((2, rows, kv_width), BF16),
            jax.ShapeDtypeStruct((prompt_rows, half), BF16),
            jax.ShapeDtypeStruct((2, out_rows, kv_width), F32),
        ],
        in_specs=[vmem] * 8 + [anywhere] * 5,
        out_specs=[vmem] * 5,
        scratch_shapes=[
            pltpu.VMEM((8, 8, responses), F32),
            pltpu.VMEM((8, 8, responses), F32),
            pltpu.VMEM((kv_heads, total, 128), BF16),
            pltpu.VMEM((kv_heads, total, 128), BF16),
            pltpu.VMEM((2, kv_heads, total, chunk), BF16),
            pltpu.VMEM((2, kv_heads, total, chunk), BF16),
            pltpu.VMEM((2, kv_heads, total, pad), BF16),
            pltpu.VMEM((2, SIDE, SIDE, 2, prompt_rows, kv_width), BF16),
            pltpu.VMEM((2, SIDE, SIDE, prompt_rows, kv_width), BF16),
            pltpu.VMEM((2, SIDE, SIDE, prompt_rows, kv_width), BF16),
            pltpu.VMEM((2, SIDE, 6) + small, BF16),
            pltpu.VMEM((2, SIDE, prompt_rows, kv_width), BF16),
            pltpu.VMEM((2, 6) + small, BF16),
            pltpu.VMEM((SIDE, SIDE, 2, prompt_rows, kv_width), BF16),
            pltpu.VMEM((SIDE, SIDE, 2, prompt_rows, kv_width), BF16),
            pltpu.VMEM((2, depth, kv_width), BF16),
            pltpu.VMEM(windows.shape, BF16),
            pltpu.VMEM((prompt_rows, half), BF16),
            pltpu.VMEM((prompt_rows, half), BF16),
            pltpu.VMEM((prompt_rows, half), F32),
            pltpu.VMEM((2, WINDOW, kv_width), F32),
            pltpu.VMEM((2, out_rows, kv_width), BF16),
            pltpu.VMEM((2, out_rows, kv_width), BF16),
            dma((3, 5)),
            dma((14,)),
            dma((14,)),
            dma((REDUCE_COPIES,)),
            dma((REDUCE_COPIES,)),
            dma((GATHER_COPIES,)),
            dma((GATHER_COPIES,)),
            dma((3,)),
            dma((3,)),
        ],
        compiler_params=params(60, collective_id=1, has_side_effects=True),
        name="backward",
    )(token_part, pick, ref_scores, q, t, inv, raw_keys, gain, e, g, kw, vw, windows)


def shards(
    prompt_hidden,
    key_weight,
    value_weight,
    key_gain,
    queries,
    response_kv,
    targets,
    ref_scores,
    lengths,
    placement_map,
):
    hidden = prompt_hidden[0]
    prompt_rows, model_width = hidden.shape
    head_width = key_gain.shape[0]
    kv_width = key_weight.shape[1]
    kv_heads = kv_width // head_width
    resp_rows = queries.shape[1]
    query_heads = queries.shape[2] // head_width
    grouped = query_heads // kv_heads
    slot_count = lengths.shape[2]
    responses = ref_scores.shape[1]
    n_ctx = lax.axis_size("ctx")
    qk_scale = 1.0 / math.sqrt(head_width)
    gain = key_gain[None]

    raw_keys, prompt_keys, prompt_values = project_and_gather(
        hidden, key_weight, value_weight, gain
    )

    ends = jnp.cumsum(lengths[0, 0], dtype=jnp.int32)
    row_ids = lax.iota(jnp.int32, resp_rows)
    slot_ids = jnp.sum(
        (row_ids[:, None] >= ends[None, :]).astype(jnp.int32), axis=1, dtype=jnp.int32
    )
    same_slot = (slot_ids[:, None] == slot_ids[None, :]) & (row_ids[None, :] <= row_ids[:, None])
    in_slot = slot_ids[:, None] == lax.iota(jnp.int32, slot_count)[None, :]
    response_ids = jnp.sum(
        jnp.where(in_slot, placement_map[0][None, :], 0), axis=1, dtype=jnp.int32
    )
    pick = (response_ids[:, None] == lax.iota(jnp.int32, responses)[None, :]).astype(F32)
    pad = -resp_rows % 128
    bias = jnp.pad(
        jnp.where(same_slot, 0.0, MASK_FILL).astype(F32),
        ((0, 0), (0, pad)),
        constant_values=MASK_FILL,
    )
    resp = jnp.pad(response_kv[0], ((0, pad), (0, 0), (0, 0)))
    q, t = queries[0], targets[0]
    e, g, inv, dq, token_part, windows = attend(
        q,
        t,
        prompt_keys,
        prompt_values,
        resp[:, 0],
        resp[:, 1],
        bias,
        hidden,
        n_ctx,
        qk_scale,
        grouped,
        2,
    )
    dpo_loss, row_grad, resp_grad, prompt_grad, weight_grad = backward(
        token_part,
        pick,
        ref_scores,
        q,
        t,
        inv,
        raw_keys,
        gain,
        e,
        g,
        key_weight,
        value_weight,
        windows,
        qk_scale,
        model_width // n_ctx // 2,
    )
    query_grad = (dq.astype(F32) * row_grad).astype(BF16)
    return (
        dpo_loss[0],
        query_grad[None],
        resp_grad.transpose(1, 0, 2)[None],
        prompt_grad[None],
        weight_grad.transpose(1, 0, 2),
    )


def solution(mesh):
    in_specs = (
        P("dp", "ctx", None),
        P(None, "tp"),
        P(None, "tp"),
        P(),
        P("dp", "ctx", "tp"),
        P("dp", "ctx", None, "tp"),
        P("dp", "ctx", "tp"),
        P("dp", None),
        P("dp", "ctx", None),
        P("dp", "ctx"),
    )
    out_specs = (
        P("dp"),
        P("dp", "ctx", "tp"),
        P("dp", "ctx", None, "tp"),
        P("dp", "ctx", "tp"),
        P(("ctx", "dp"), None, "tp"),
    )
    return jax.shard_map(shards, mesh=mesh, in_specs=in_specs, out_specs=out_specs, check_vma=False)
```

time: 448 us -> 143 us (0.32)
  waiting for transfers between devices: 183 us -> 0 us
  blocking collectives: 163 us -> 0 us
  Pallas kernels: 44.5 us -> 132 us
  matrix products: 17.5 us -> 0 us
  local copies, waits for them, and re-layouts: 19.9 us -> 4.95 us
  between operations: 14.1 us -> 2.55 us
    psum x1 -> x0, blocking collectives: 138 us -> none  [shards(): lax.psum(jnp.sum(slot_part[:, None] * place_onehot, axis=0), ('ctx', 'tp'))]
    reduce_scatter x3 -> x0, waiting for transfers between devices: 107 us -> none  [the longest x1 79.9 us: shards(): lax.psum_scatter(dkv, 'ctx', scatter_dimension=1, tiled=True).astype(F32)]
    pallas_call x1 -> x2, Pallas kernels: 14.3 us -> 97.7 us  [the longest x1 64.2 us: backward(): pl.pallas_call(functools.partial(backward_kernel, scale), out_shape=[jax....]
    all_gather x2 -> x0, waiting for transfers between devices: 75.5 us -> none  [the longest x1 49.7 us: shards(): lax.all_gather(jnp.stack([prompt_keys, prompt_values], axis=0), 'ctx', ax...]
    all_to_all x1 -> x0, blocking collectives: 25.4 us -> none  [shards(): lax.all_to_all(hidden.reshape(prompt_rows, n_ctx, model_width // n_ctx).t...]
    dot_general x6 -> x0, matrix products: 17.5 us -> none  [the longest x1 5.05 us: shards(): lax.dot_general(kv_grad_b[1], value_weight, NT, preferred_element_type=F32)]
    dot_general x1 -> x0, local copies, waits for them, and re-layouts: 7.91 us -> none  [shards(): jnp.dot(hidden, key_weight, preferred_element_type=F32)]
  transfers between devices with their start and end apart: 5 -> 0, of which waited for: 5 -> 0; matrix products, arithmetic and copies ran while one was open for 3% -> 0% of each run, Pallas kernels for 0% -> 0%
where the time goes in v2:
time: 143 us
  Pallas kernels  132 us (92%)
  local copies, waits for them, and re-layouts  4.95 us (3%)
  other arithmetic  3.21 us (2%)
  between operations  2.55 us (2%)
    pallas_call x1, Pallas kernels, backward(): pl.pallas_call(functools.partial(backward_kernel, scale), out_shape=[jax....  64.2 us
    pallas_call x1, Pallas kernels, attend(): pl.pallas_call(functools.partial(attend_kernel, scale), grid=(kv_heads, s...  34.2 us
    pallas_call x1, Pallas kernels, project_and_gather(): pl.pallas_call(project_kernel, out_shape=[jax.ShapeDtypeStruct((rows, wid...  33.5 us
    unnamed x16, local copies, waits for them, and re-layouts  3.6 us

profile of v2, /device:TPU:1, one launch (start us, length us, event | category | flops | bytes accessed | tf_op | source)
XLA Modules:
  0.0 142.6 jit_solution(3919431839695641716)
XLA Ops:
  0.6 0.0 copy-start.2
  0.6 0.0 copy-start.4
  0.7 33.5 %project_and_gather.1 = (f32[64,512]{1,0:T(8,128)}, bf16[4,4,2,64,512]{4,3,2,1,0:T(8,128)(2,1)}, bf16[4,4,2,64,512]{4,3,2,1,0:T(8,128)(2,1)}) custom-call(bf16[64,5120]{1,0:T(8,128)(2,1)} %bitcast.28, bf16[5120,512]{1,0:T(8,128)(2,1)} %kw_ref.3, bf16[5120,512]{1,0:T(8,128)(2,1)} %vw_ref.3, f32[1,128]{1,0:T(1,128)} %bitcast.36), custom_call_target="tpu_custom_call" | custom-call | tf_op jit(solution)/shard_map/project_and_gather/pallas_call | solution.py:250
  34.2 0.0 copy-done.2
  34.2 0.7 fusion.2
  34.9 0.0 copy-done.4
  34.9 0.2 reduce-window.8
  35.1 0.1 convert_reduce_fusion
  35.2 0.1 fusion.5
  35.3 0.6 pad.9.bias_ref
  35.9 0.0 copy-start.5
  35.9 34.2 %attend.1 = (bf16[4,768,2176]{2,1,0:T(8,128)(2,1)}, bf16[4,768,2176]{2,1,0:T(8,128)(2,1)}, f32[4,768,1]{2,1,0:T(8,128)}, bf16[96,4096]{1,0:T(8,128)(2,1)}, f32[9...) custom-call(bf16[96,4096]{1,0:T(8,128)(2,1)} %bitcast.24, bf16[96,4096]{1,0:T(8,128)(2,1)} %bitcast.26, ...), custom_call_target="tpu_custom_call" | custom-call | tf_op jit(solution)/shard_map/attend/pallas_call | solution.py:403
  70.1 0.0 copy-done.5
  70.1 0.1 select_reduce_fusion
  70.2 0.7 fusion.3.pick_ref
  70.9 0.0 copy-start
  70.9 64.2 %backward.1 = (f32[1,1]{1,0:T(1,128)}, f32[96,1]{1,0:T(8,128)}, bf16[2,96,512]{2,1,0:T(8,128)(2,1)}, bf16[64,2560]{1,0:T(8,128)(2,1)}, f32[2,80,512]{2,1,0:T(8,128)}) custom-call(f32[96,1]{1,0:T(8,128)} %get-tuple-element.21.token_ref, f32[96,256]{1,0:T(8,128)} %fusion.3.pick_ref, f32[1,256]{1,0:T(1,128)} %ref_ref.1, bf16[96,4096]{1,0:T(8,128)(2,1)} %bitcast.25, ...), custom_call_target="tpu_custom_call" | custom-call | tf_op jit(solution)/shard_map/backward/pallas_call | solution.py:817
  135.1 0.0 copy-start.3
  135.2 0.0 copy-start.1
  135.2 1.0 reduce
  136.1 0.0 copy-done
  136.1 1.1 fusion
  137.2 1.9 %copy.23 = f32[80,2,512]{2,1,0:T(2,128)} copy(f32[80,2,512]{2,0,1:T(8,128)} %bitcast.34) | data formatting | bytes 655360
  139.2 0.0 copy-done.3
  139.2 0.9 copy.22
  140.7 0.0 copy-done.1
  140.8 0.7 copy.29
  (1 shorter events, 0.0 us)
Async XLA Ops:
  0.6 33.5 %copy-start.2 = (bf16[1,96,2,512]{3,2,1,0:T(2,128)(2,1)S(1)}, bf16[1,96,2,512]{3,2,1,0:T(2,128)(2,1)}, u32[]{:S(2)}) copy-start(bf16[1,96,2,512]{3,2,1,0:T(2,128)(2,1)} %param.15) | copy-start | bytes 589828
  0.6 34.3 %copy-start.4 = (s32[1,1,8]{2,1,0:T(1,128)S(1)}, s32[1,1,8]{2,1,0:T(1,128)}, u32[]{:S(2)}) copy-start(s32[1,1,8]{2,1,0:T(1,128)} %param.18) | copy-start | bytes 100
  35.9 34.2 %copy-start.5 = (s32[1,8]{1,0:T(1,128)S(1)}, s32[1,8]{1,0:T(1,128)}, u32[]{:S(2)}) copy-start(s32[1,8]{1,0:T(1,128)} %param.19) | copy-start | bytes 100
  70.9 65.2 %copy-start = (bf16[96,4096]{1,0:T(8,128)(2,1)S(1)}, bf16[96,4096]{1,0:T(8,128)(2,1)}, u32[]{:S(2)}) copy-start(bf16[96,4096]{1,0:T(8,128)(2,1)} %get-tuple-element.28) | copy-start | bytes 2359300
  135.1 4.0 %copy-start.3 = (bf16[2,96,512]{2,1,0:T(8,128)(2,1)S(1)}, bf16[2,96,512]{2,1,0:T(8,128)(2,1)}, u32[]{:S(2)}) copy-start(bf16[2,96,512]{2,1,0:T(8,128)(2,1)} %get-tuple-element.30) | copy-start | bytes 589828
  135.2 5.6 %copy-start.1 = (bf16[64,2560]{1,0:T(8,128)(2,1)S(1)}, bf16[64,2560]{1,0:T(8,128)(2,1)}, u32[]{:S(2)}) copy-start(bf16[64,2560]{1,0:T(8,128)(2,1)} %get-tuple-element.31) | copy-start | bytes 983044

commit v3 on v2

--- a/solution.py
+++ b/solution.py
@@ -265,15 +265,37 @@
     return raw, keys.reshape(total, width), values.reshape(total, width)
 
 
+def slots_of(lengths_ref, ids):
+    slots, end = jnp.zeros(ids.shape, jnp.int32), 0
+    for i in range(lengths_ref.shape[0]):
+        end = end + lengths_ref[i]
+        slots = slots + jnp.where(ids >= end, 1, 0)
+    return slots
+
+
+def slot_bias(lengths_ref, rows, pad):
+    row = lax.broadcasted_iota(jnp.int32, (rows, pad), 0)
+    key = lax.broadcasted_iota(jnp.int32, (rows, pad), 1)
+    seen = (slots_of(lengths_ref, row) == slots_of(lengths_ref, key)) & (key <= row)
+    return jnp.where(seen, 0.0, MASK_FILL)
+
+
+def response_pick(lengths_ref, map_ref, rows, responses):
+    slots = slots_of(lengths_ref, lax.broadcasted_iota(jnp.int32, (rows, responses), 0))
+    ids = jnp.zeros((rows, responses), jnp.int32)
+    for i in range(map_ref.shape[0]):
+        ids = jnp.where(slots == i, map_ref[i], ids)
+    return jnp.where(ids == lax.broadcasted_iota(jnp.int32, (rows, responses), 1), 1.0, 0.0)
+
+
 def attend_kernel(
     scale,
     q_ref,
     t_ref,
     k_ref,
     v_ref,
-    rk_ref,
-    rv_ref,
-    bias_ref,
+    r_ref,
+    lengths_ref,
     h_ref,
     e_ref,
     g_ref,
@@ -323,51 +345,82 @@
         pl.semaphore_wait(barrier, n - 1)
         lax.fori_loop(1, n, go, 0)
         own_copy.start()
-
-    heads = q_ref.shape[1] // 128
-    rows = q_ref.shape[0]
-    q = jnp.concatenate([q_ref[:, i * 128 : (i + 1) * 128] for i in range(heads)], axis=0)
-    t = jnp.concatenate([t_ref[:, i * 128 : (i + 1) * 128] for i in range(heads)], axis=0)
-    bias = jnp.concatenate([bias_ref[...]] * heads, axis=0)
-    k, v, rk, rv = k_ref[...], v_ref[...], rk_ref[...], rv_ref[...]
-    s = lax.dot_general(q, k, NT, preferred_element_type=F32)
-    sr = lax.dot_general(q, rk, NT, preferred_element_type=F32) + bias
-    peak = jnp.maximum(
-        jnp.max(s, axis=1, keepdims=True), jnp.max(sr, axis=1, keepdims=True)
-    )
+        tok_ref[...] = jnp.zeros_like(tok_ref)
+
+    rows, heads = q_ref.shape[0], q_ref.shape[1] // 128
+    tokens = k_ref.shape[0]
+    pad = -rows % 128
+    filler = jnp.zeros((pad, 128), BF16)
+    k, v = k_ref[...], v_ref[...]
+    rk = jnp.concatenate([r_ref[0], filler], axis=0)
+    rv = jnp.concatenate([r_ref[1], filler], axis=0)
+    bias = slot_bias(lengths_ref, rows, rows + pad)
     factor = scale * LOG2E
-    top = peak * factor
-    e = jnp.exp2(s * factor - top)
-    er = jnp.exp2(sr * factor - top)
-    inv = 1.0 / (jnp.sum(e, axis=1, keepdims=True) + jnp.sum(er, axis=1, keepdims=True))
-    eb, erb = e.astype(BF16), er.astype(BF16)
-    tokens = k.shape[0]
-    e_ref[0, :, :tokens] = eb
-    e_ref[0, :, tokens:] = erb
-    attended = (
-        jnp.dot(eb, v, preferred_element_type=F32) + jnp.dot(erb, rv, preferred_element_type=F32)
-    ) * inv
-    dot = jnp.sum(attended * t.astype(F32), axis=1, keepdims=True)
-    dp = lax.dot_general(t, v, NT, preferred_element_type=F32)
-    dpr = lax.dot_general(t, rv, NT, preferred_element_type=F32)
-    gb = (eb.astype(F32) * (dp - dot)).astype(BF16)
-    grb = (erb.astype(F32) * (dpr - dot)).astype(BF16)
-    g_ref[0, :, :tokens] = gb
-    g_ref[0, :, tokens:] = grb
-    dq = (
-        jnp.dot(gb, k, preferred_element_type=F32) + jnp.dot(grb, rk, preferred_element_type=F32)
-    ) * (inv * scale)
-    inv_ref[0] = inv
-    for i in range(heads):
-        dq_ref[:, i * 128 : (i + 1) * 128] = dq[i * rows : (i + 1) * rows].astype(BF16)
-
-    @pl.when((pl.program_id(0) == 0) & (pl.program_id(1) == 0))
-    def _():
-        tok_ref[...] = jnp.zeros_like(tok_ref)
-
-    total = dot[:rows]
-    for i in range(1, heads):
-        total = total + dot[i * rows : (i + 1) * rows]
+    parts = range(0, heads, 2)
+    bias = jnp.concatenate([bias, bias], axis=0)
+
+    def two(ref, i):
+        return jnp.concatenate([ref[:, i * 128 : (i + 1) * 128], ref[:, (i + 1) * 128 : (i + 2) * 128]], axis=0)
+
+    def out_rows(i):
+        return slice(i * rows, (i + 2) * rows)
+
+    def logits(i):
+        q = two(q_ref, i)
+        s = lax.dot_general(q, k, NT, preferred_element_type=F32)
+        return s, lax.dot_general(q, rk, NT, preferred_element_type=F32) + bias
+
+    def weigh(i, s, sr):
+        peak = jnp.maximum(
+            jnp.max(s, axis=1, keepdims=True), jnp.max(sr, axis=1, keepdims=True)
+        )
+        top = peak * factor
+        e = jnp.exp2(s * factor - top)
+        er = jnp.exp2(sr * factor - top)
+        inv = 1.0 / (
+            jnp.sum(e, axis=1, keepdims=True) + jnp.sum(er, axis=1, keepdims=True)
+        )
+        e_ref[0, out_rows(i), :tokens] = e.astype(BF16)
+        e_ref[0, out_rows(i), tokens:] = er.astype(BF16)
+        inv_ref[0, out_rows(i)] = inv
+        return inv
+
+    def read(i, inv):
+        t = two(t_ref, i)
+        e, er = e_ref[0, out_rows(i), :tokens], e_ref[0, out_rows(i), tokens:]
+        dp = lax.dot_general(t, v, NT, preferred_element_type=F32)
+        dpr = lax.dot_general(t, rv, NT, preferred_element_type=F32)
+        attended = jnp.dot(e, v, preferred_element_type=F32)
+        attended = (attended + jnp.dot(er, rv, preferred_element_type=F32)) * inv
+        dot = jnp.sum(attended * t.astype(F32), axis=1, keepdims=True)
+        return dp, dpr, dot
+
+    def differ(i, dp, dpr, dot):
+        e, er = e_ref[0, out_rows(i), :tokens], e_ref[0, out_rows(i), tokens:]
+        g_ref[0, out_rows(i), :tokens] = (e.astype(F32) * (dp - dot)).astype(BF16)
+        g_ref[0, out_rows(i), tokens:] = (er.astype(F32) * (dpr - dot)).astype(BF16)
+
+    def query_grad(i, inv):
+        g, gr = g_ref[0, out_rows(i), :tokens], g_ref[0, out_rows(i), tokens:]
+        dq = jnp.dot(g, k, preferred_element_type=F32)
+        dq = (dq + jnp.dot(gr, rk, preferred_element_type=F32)) * (inv * scale)
+        dq_ref[:, i * 128 : (i + 1) * 128] = dq[:rows].astype(BF16)
+        dq_ref[:, (i + 1) * 128 : (i + 2) * 128] = dq[rows:].astype(BF16)
+
+    scores = {i: logits(i) for i in parts}
+    invs, reads, total = {}, {}, jnp.zeros((rows, 1), F32)
+    for i in parts:
+        invs[i] = weigh(i, *scores[i])
+        reads[i] = read(i, invs[i])
+        if i >= 2:
+            differ(i - 2, *reads[i - 2])
+            query_grad(i - 2, invs[i - 2])
+    last = heads - 2
+    differ(last, *reads[last])
+    query_grad(last, invs[last])
+    for i in parts:
+        dot = reads[i][2]
+        total = total + dot[:rows] + dot[rows:]
     tok_ref[...] += total
 
     @pl.when(
@@ -385,17 +438,16 @@
 WINDOW = 256
 
 
-def attend(q, t, prompt_keys, prompt_values, rk, rv, bias, hidden, n, scale, grouped, chunk):
+def attend(q, t, prompt_keys, prompt_values, resp, lengths, hidden, n, scale, grouped, chunk):
     rows = q.shape[0]
     tokens, kv_width = prompt_keys.shape
     kv_heads = kv_width // 128
-    pad = rk.shape[0]
+    pad = rows + -rows % 128
     steps = grouped // chunk
     m = chunk * rows
     total = grouped * rows
     row_block = pl.BlockSpec((rows, chunk * 128), lambda h, c: (0, h * steps + c))
     head_block = pl.BlockSpec((tokens, 128), lambda h, c: (0, h))
-    resp_block = pl.BlockSpec((pad, 128), lambda h, c: (0, h))
 
     def score_block(width):
         return pl.BlockSpec((1, m, width), lambda h, c: (h, c, 0))
@@ -408,9 +460,8 @@
             row_block,
             head_block,
             head_block,
-            resp_block,
-            resp_block,
-            pl.BlockSpec((rows, pad), lambda h, c: (0, 0)),
+            pl.BlockSpec((2, rows, 128), lambda h, c: (0, 0, h)),
+            pl.BlockSpec(memory_space=pltpu.SMEM),
             pl.BlockSpec(memory_space=pl.ANY),
         ],
         out_specs=[
@@ -436,7 +487,7 @@
         ],
         compiler_params=params(56, collective_id=3, has_side_effects=True),
         name="attend",
-    )(q, t, prompt_keys, prompt_values, rk, rv, bias, hidden)
+    )(q, t, prompt_keys, prompt_values, resp, lengths, hidden)
 
 
 def norm_backward(raw, gain, grad):
@@ -555,11 +606,13 @@
 def backward_kernel(
     scale,
     token_ref,
-    pick_ref,
+    lengths_ref,
+    map_ref,
     ref_ref,
     q_ref,
     t_ref,
     inv_ref,
+    dq_ref,
     raw_ref,
     gain_ref,
     e_ref,
@@ -568,7 +621,7 @@
     vw_ref,
     hw_ref,
     loss_ref,
-    row_ref,
+    qgrad_ref,
     resp_ref,
     pgrad_ref,
     wgrad_ref,
@@ -668,7 +721,7 @@
     other_dp = {"dp": 1 - dp}
     greet([first(k) for k in range(1, 8)] + [second(k) for k in range(1, 8)] + [other_dp])
     score_copies = Copies(score_send, score_recv)
-    pick = pick_ref[...]
+    pick = response_pick(lengths_ref, map_ref, rows, ref_ref.shape[1])
     part = jnp.sum(pick * token_ref[...], axis=0, keepdims=True)
     one_ref[x * 2 + tp] = jnp.broadcast_to(part, one_ref.shape[1:])
     half_sum = share_scores(one_ref, x * 2 + tp, first, score_copies, 0)
@@ -681,7 +734,6 @@
     pair_grad = -DPO_BETA * jnp.where(margin >= 0.0, small, 1.0) / (1.0 + small)
     score_grad = jnp.concatenate([pair_grad, -pair_grad], axis=1)
     row_grad = jnp.sum(pick * score_grad, axis=1, keepdims=True)
-    row_ref[...] = row_grad
     row_factor = jnp.concatenate([row_grad] * grouped, axis=0)
     start(more)
     for h in range(kv_heads):
@@ -732,6 +784,7 @@
         for h in range(kv_heads):
             grads = lax.dot_general(rbuf_ref[kv, h], scaled[h], TN, preferred_element_type=F32)
             resp_ref[kv, :, h * 128 : (h + 1) * 128] = grads[:rows].astype(BF16)
+    qgrad_ref[...] = (dq_ref[...].astype(F32) * row_grad).astype(BF16)
     loss = jnp.maximum(-margin, 0.0) + jnp.log1p(small)
     loss_ref[...] = jnp.sum(loss, axis=1, keepdims=True)
     for kv in range(2):
@@ -780,7 +833,7 @@
     last_copies.arrived(pcame_ref, 0)
     pgrad_ref[...] = (pown_ref[...] + pcame_ref[...].astype(F32)).astype(BF16)
 
-    out_rows = wgrad_ref.shape[1]
+    out_rows = wgrad_ref.shape[0]
     shift = (ctx % 4) * 32
     hidden = h_ref[...].reshape(-1, h_ref.shape[2])
     for kv, ref in enumerate((gk_ref, gv_ref)):
@@ -795,14 +848,30 @@
     own = pl.ds(pl.multiple_of(shift + dp * out_rows, 16), out_rows)
     for kv in range(2):
         last_copies.arrived(wcame_ref.at[kv], 1 + kv)
-        wgrad_ref[kv] = wpart_ref[kv, own] + wcame_ref[kv].astype(F32)
+        wgrad_ref[:, kv] = wpart_ref[kv, own] + wcame_ref[kv].astype(F32)
     last_copies.finish()
 
 
 def backward(
-    token_part, pick, ref_scores, q, t, inv, raw_keys, gain, e, g, kw, vw, windows, scale, out_rows
+    token_part,
+    lengths,
+    places,
+    ref_scores,
+    q,
+    t,
+    inv,
+    dq,
+    raw_keys,
+    gain,
+    e,
+    g,
+    kw,
+    vw,
+    windows,
+    scale,
+    out_rows,
 ):
-    rows, responses = pick.shape
+    rows, responses = q.shape[0], ref_scores.shape[1]
     kv_heads, total, width = e.shape
     prompt_rows, kv_width = raw_keys.shape
     depth = kw.shape[0]
@@ -812,18 +881,19 @@
     chunk = tokens // SIDE
     half = depth // 2
     vmem, anywhere = pl.BlockSpec(memory_space=pltpu.VMEM), pl.BlockSpec(memory_space=pl.ANY)
+    smem = pl.BlockSpec(memory_space=pltpu.SMEM)
     dma = pltpu.SemaphoreType.DMA
     small = (prompt_rows // 2, kv_width)
     return pl.pallas_call(
         functools.partial(backward_kernel, scale),
         out_shape=[
             jax.ShapeDtypeStruct((1, 1), F32),
-            jax.ShapeDtypeStruct((rows, 1), F32),
+            jax.ShapeDtypeStruct(q.shape, BF16),
             jax.ShapeDtypeStruct((2, rows, kv_width), BF16),
             jax.ShapeDtypeStruct((prompt_rows, half), BF16),
-            jax.ShapeDtypeStruct((2, out_rows, kv_width), F32),
+            jax.ShapeDtypeStruct((out_rows, 2, kv_width), F32),
         ],
-        in_specs=[vmem] * 8 + [anywhere] * 5,
+        in_specs=[vmem, smem, smem] + [vmem] * 7 + [anywhere] * 5,
         out_specs=[vmem] * 5,
         scratch_shapes=[
             pltpu.VMEM((8, 8, responses), F32),
@@ -861,7 +931,23 @@
         ],
         compiler_params=params(60, collective_id=1, has_side_effects=True),
         name="backward",
-    )(token_part, pick, ref_scores, q, t, inv, raw_keys, gain, e, g, kw, vw, windows)
+    )(
+        token_part,
+        lengths,
+        places,
+        ref_scores,
+        q,
+        t,
+        inv,
+        dq,
+        raw_keys,
+        gain,
+        e,
+        g,
+        kw,
+        vw,
+        windows,
+    )
 
 
 def shards(
@@ -881,11 +967,8 @@
     head_width = key_gain.shape[0]
     kv_width = key_weight.shape[1]
     kv_heads = kv_width // head_width
-    resp_rows = queries.shape[1]
     query_heads = queries.shape[2] // head_width
     grouped = query_heads // kv_heads
-    slot_count = lengths.shape[2]
-    responses = ref_scores.shape[1]
     n_ctx = lax.axis_size("ctx")
     qk_scale = 1.0 / math.sqrt(head_width)
     gain = key_gain[None]
@@ -894,46 +977,30 @@
         hidden, key_weight, value_weight, gain
     )
 
-    ends = jnp.cumsum(lengths[0, 0], dtype=jnp.int32)
-    row_ids = lax.iota(jnp.int32, resp_rows)
-    slot_ids = jnp.sum(
-        (row_ids[:, None] >= ends[None, :]).astype(jnp.int32), axis=1, dtype=jnp.int32
-    )
-    same_slot = (slot_ids[:, None] == slot_ids[None, :]) & (row_ids[None, :] <= row_ids[:, None])
-    in_slot = slot_ids[:, None] == lax.iota(jnp.int32, slot_count)[None, :]
-    response_ids = jnp.sum(
-        jnp.where(in_slot, placement_map[0][None, :], 0), axis=1, dtype=jnp.int32
-    )
-    pick = (response_ids[:, None] == lax.iota(jnp.int32, responses)[None, :]).astype(F32)
-    pad = -resp_rows % 128
-    bias = jnp.pad(
-        jnp.where(same_slot, 0.0, MASK_FILL).astype(F32),
-        ((0, 0), (0, pad)),
-        constant_values=MASK_FILL,
-    )
-    resp = jnp.pad(response_kv[0], ((0, pad), (0, 0), (0, 0)))
+    resp = response_kv[0].transpose(1, 0, 2)
     q, t = queries[0], targets[0]
     e, g, inv, dq, token_part, windows = attend(
         q,
         t,
         prompt_keys,
         prompt_values,
-        resp[:, 0],
-        resp[:, 1],
-        bias,
+        resp,
+        lengths[0, 0],
         hidden,
         n_ctx,
         qk_scale,
         grouped,
-        2,
+        4,
     )
-    dpo_loss, row_grad, resp_grad, prompt_grad, weight_grad = backward(
+    dpo_loss, query_grad, resp_grad, prompt_grad, weight_grad = backward(
         token_part,
-        pick,
+        lengths[0, 0],
+        placement_map[0],
         ref_scores,
         q,
         t,
         inv,
+        dq,
         raw_keys,
         gain,
         e,
@@ -944,13 +1011,12 @@
         qk_scale,
         model_width // n_ctx // 2,
     )
-    query_grad = (dq.astype(F32) * row_grad).astype(BF16)
     return (
-        dpo_loss[0],
+        dpo_loss.reshape(1),
         query_grad[None],
         resp_grad.transpose(1, 0, 2)[None],
         prompt_grad[None],
-        weight_grad.transpose(1, 0, 2),
+        weight_grad,
     )
 
 

time: 143 us -> 138 us (0.965)
  Pallas kernels: 132 us -> 126 us
  local copies, waits for them, and re-layouts: 4.95 us -> 8.93 us
  other arithmetic: 3.21 us -> 0 us
    pallas_call x1, Pallas kernels: 34.2 us -> 26.6 us  [attend(): pl.pallas_call(functools.partial(attend_kernel, scale), grid=(kv_heads, s...]
    unnamed x16 -> x5, local copies, waits for them, and re-layouts: 3.6 us -> 8.93 us
    pallas_call x1, Pallas kernels: 64.2 us -> 66.1 us  [backward(): pl.pallas_call(functools.partial(backward_kernel, scale), out_shape=[jax....]
where the time goes in v3:
time: 138 us; the launch traced here: 137 us
  Pallas kernels  126 us (91%)
  local copies, waits for them, and re-layouts  8.93 us (6%)
  between operations  2.35 us (2%)
    pallas_call x1, Pallas kernels, backward(): pl.pallas_call(functools.partial(backward_kernel, scale), out_shape=[jax....  66.1 us
    pallas_call x1, Pallas kernels, project_and_gather(): pl.pallas_call(project_kernel, out_shape=[jax.ShapeDtypeStruct((rows, wid...  33.4 us
    pallas_call x1, Pallas kernels, attend(): pl.pallas_call(functools.partial(attend_kernel, scale), grid=(kv_heads, s...  26.6 us
    unnamed x5, local copies, waits for them, and re-layouts  8.93 us

profile of v3, /device:TPU:1, one launch (start us, length us, event | category | flops | bytes accessed | tf_op | source)
XLA Modules:
  0.0 137.4 jit_solution(11840400597987570529)
XLA Ops:
  0.6 1.6 %copy.18 = bf16[1,96,2,512]{3,1,2,0:T(8,128)(2,1)} copy(bf16[1,96,2,512]{3,2,1,0:T(2,128)(2,1)} %param.15) | data formatting | bytes 393216 | tf_op args[5]
  2.3 33.4 %project_and_gather.1 = (f32[64,512]{1,0:T(8,128)}, bf16[4,4,2,64,512]{4,3,2,1,0:T(8,128)(2,1)}, bf16[4,4,2,64,512]{4,3,2,1,0:T(8,128)(2,1)}) custom-call(bf16[64,5120]{1,0:T(8,128)(2,1)} %bitcast.23, bf16[5120,512]{1,0:T(8,128)(2,1)} %kw_ref.3, bf16[5120,512]{1,0:T(8,128)(2,1)} %vw_ref.3, f32[1,128]{1,0:T(1,128)} %bitcast.31), custom_call_target="tpu_custom_call" | custom-call | tf_op jit(solution)/shard_map/project_and_gather/pallas_call | solution.py:250
  35.7 26.6 %attend.1 = (bf16[4,768,2176]{2,1,0:T(8,128)(2,1)}, bf16[4,768,2176]{2,1,0:T(8,128)(2,1)}, f32[4,768,1]{2,1,0:T(8,128)}, bf16[96,4096]{1,0:T(8,128)(2,1)}, f32[9...) custom-call(bf16[96,4096]{1,0:T(8,128)(2,1)} %bitcast.19, bf16[96,4096]{1,0:T(8,128)(2,1)} %bitcast.21, ...), custom_call_target="tpu_custom_call" | custom-call | tf_op jit(solution)/shard_map/attend/pallas_call | solution.py:455
  62.3 66.1 %backward.1 = (f32[1,1]{1,0:T(1,128)}, bf16[96,4096]{1,0:T(8,128)(2,1)}, bf16[2,96,512]{2,1,0:T(8,128)(2,1)}, bf16[64,2560]{1,0:T(8,128)(2,1)}, f32[80,2,512]{2,1,0:T(2,128)}) custom-call(f32[96,1]{1,0:T(8,128)} %get-tuple-element.21.token_ref, s32[8]{0:T(128)} %bitcast.34, s32[8]{0:T(128)} %bitcast.35, f32[1,256]{1,0:T(1,128)} %ref_ref.1, ...), custom_call_target="tpu_custom_call" | custom-call | tf_op jit(solution)/shard_map/backward/pallas_call | solution.py:887
  128.4 1.8 %copy.16 = bf16[1,96,2,512]{3,2,1,0:T(2,128)(2,1)} copy(bf16[1,96,2,512]{3,1,2,0:T(8,128)(2,1)} %bitcast.30) | data formatting | bytes 393216
  130.8 2.1 %copy.24 = bf16[1,96,4096]{2,1,0:T(8,128)(2,1)} copy(bf16[1,96,4096]{2,1,0:T(8,128)(2,1)} %bitcast.27) | data formatting | bytes 1572864
  132.8 1.7 %copy.25 = bf16[1,64,2560]{2,1,0:T(8,128)(2,1)} copy(bf16[1,64,2560]{2,1,0:T(8,128)(2,1)} %bitcast.29) | data formatting | bytes 655360
  134.5 1.7 %copy.26 = f32[80,2,512]{2,1,0:T(2,128)} copy(f32[80,2,512]{2,1,0:T(2,128)} %get-tuple-element.47) | data formatting | bytes 655360

commit v4 on v3

--- a/solution.py
+++ b/solution.py
@@ -67,6 +67,7 @@
 class Copies:
     def __init__(self, send_sem, recv_sem):
         self.send_sem, self.recv_sem, self.started = send_sem, recv_sem, []
+        self.draining = False
 
     def make(self, src, dst, peer, slot):
         return pltpu.make_async_remote_copy(
@@ -80,10 +81,15 @@
 
     def send(self, src, dst, peer, slot):
         one = self.make(src, dst, peer, slot)
+        if self.draining:
+            one.wait_send()
+            return
         one.start()
         self.started.append(one)
 
     def arrived(self, dst, slot):
+        if self.draining:
+            return
         x, z, core = place()
         self.make(dst, dst, ctx_id(x, z, 1 - core), slot).wait_recv()
 
@@ -92,177 +98,82 @@
             one.wait_send()
 
 
-GATHER_COPIES = 72
-
-
-def gather_stages(refs, copies):
+GATHER_COPIES = 24
+
+
+def gather_stages(ref_of, rows, copies, base):
     x, z, core = place()
     partner = ctx_id(x, z, 1 - core)
-    rows = refs[0].shape[3]
     full, low, high = pl.ds(0, rows), pl.ds(0, rows // 2), pl.ds(rows // 2, rows // 2)
     rings = {}
     for kv in range(2):
-        for level in range(2):
-            p, at = ring(kv if level == 0 else 1 - kv)
+        for phase in range(2):
+            p, at = ring(kv if phase == 0 else 1 - kv)
             right, left, opposite = around(p)
-            rings[kv, level] = ((p, left, right, opposite), at(right), at(left))
-
-    def block(kv, i, j, part=full, of_core=None):
-        of_core = core if of_core is None else of_core
-        i, j = rings[kv, 0][0][i], rings[kv, 1][0][j]
-        spot = (i, j) if kv == 0 else (j, i)
-        return refs[kv].at[spot[0], spot[1], of_core, part]
-
-    def first(kv, k):
-        return kv * 36 + k
-
-    def second(kv, i, k):
-        return kv * 36 + 4 + i * 4 + k
-
-    def swap_slot(kv, i, j):
-        return kv * 36 + 20 + i * 4 + j
-
-    def send(ref, peer, slot):
-        copies.send(ref, ref, peer, slot)
-
-    def to_core(kv, i, j):
-        send(block(kv, i, j), partner, swap_slot(kv, i, j))
-
-    def onward(kv, i):
-        _, right, left = rings[kv, 1]
-        send(block(kv, i, 0), right, second(kv, i, 0))
-        send(block(kv, i, 0), left, second(kv, i, 1))
-        to_core(kv, i, 0)
-
-    def open_all():
+            rings[kv, phase] = ((p, left, right, opposite), at(right), at(left))
+
+    def block(kv, phase, i, part=full, of_core=core):
+        p = rings[kv, phase][0][i]
+        if phase == 1:
+            x_at, z_at = (slice(None), p) if kv == 0 else (p, slice(None))
+        else:
+            x_at, z_at = (p, z) if kv == 0 else (x, p)
+        return ref_of(kv).at[:, x_at, z_at, of_core, part]
+
+    def slot(kv, phase, k):
+        return base + (kv * 2 + phase) * 4 + k
+
+    def send(ref, peer, at):
+        copies.send(ref, ref, peer, at)
+
+    def to_core(kv, i):
+        send(block(kv, 1, i), partner, base + 16 + kv * 4 + i)
+
+    def start(phase):
         for kv in range(2):
-            _, right, left = rings[kv, 0]
-            send(block(kv, 0, 0), right, first(kv, 0))
-            send(block(kv, 0, 0), left, first(kv, 1))
+            _, right, left = rings[kv, phase]
+            send(block(kv, phase, 0), right, slot(kv, phase, 0))
+            send(block(kv, phase, 0), left, slot(kv, phase, 1))
+        if phase == 1:
+            for kv in range(2):
+                to_core(kv, 0)
+
+    def forward(phase):
         for kv in range(2):
-            onward(kv, 0)
-
-    def first_neighbours():
+            _, right, left = rings[kv, phase]
+            copies.arrived(block(kv, phase, 1), slot(kv, phase, 0))
+            send(block(kv, phase, 1, low), right, slot(kv, phase, 2))
+            copies.arrived(block(kv, phase, 2), slot(kv, phase, 1))
+            send(block(kv, phase, 2, high), left, slot(kv, phase, 3))
+        if phase == 1:
+            for kv in range(2):
+                to_core(kv, 1)
+                to_core(kv, 2)
+
+    def close(phase):
         for kv in range(2):
-            _, right, left = rings[kv, 0]
-            copies.arrived(block(kv, 1, 0), first(kv, 0))
-            send(block(kv, 1, 0, low), right, first(kv, 2))
-            onward(kv, 1)
-            copies.arrived(block(kv, 2, 0), first(kv, 1))
-            send(block(kv, 2, 0, high), left, first(kv, 3))
-            onward(kv, 2)
-
-    def first_opposite():
+            copies.arrived(block(kv, phase, 3, low), slot(kv, phase, 2))
+            copies.arrived(block(kv, phase, 3, high), slot(kv, phase, 3))
+            if phase == 1:
+                to_core(kv, 3)
+
+    def turn():
+        close(0)
+        start(1)
+
+    def from_core():
         for kv in range(2):
-            copies.arrived(block(kv, 3, 0, low), first(kv, 2))
-            copies.arrived(block(kv, 3, 0, high), first(kv, 3))
-            onward(kv, 3)
-
-    def second_neighbours(i):
-        for kv in range(2):
-            _, right, left = rings[kv, 1]
-            copies.arrived(block(kv, i, 1), second(kv, i, 0))
-            send(block(kv, i, 1, low), right, second(kv, i, 2))
-            to_core(kv, i, 1)
-            copies.arrived(block(kv, i, 2), second(kv, i, 1))
-            send(block(kv, i, 2, high), left, second(kv, i, 3))
-            to_core(kv, i, 2)
-
-    def second_opposite(i):
-        for kv in range(2):
-            copies.arrived(block(kv, i, 3, low), second(kv, i, 2))
-            copies.arrived(block(kv, i, 3, high), second(kv, i, 3))
-            to_core(kv, i, 3)
-
-    def from_core(kv):
-        for i in range(4):
-            for j in range(4):
-                copies.arrived(block(kv, i, j, full, 1 - core), swap_slot(kv, i, j))
+            for i in range(4):
+                copies.arrived(block(kv, 1, i, full, 1 - core), base + 16 + kv * 4 + i)
 
     return [
-        open_all,
-        first_neighbours,
-        lambda: second_neighbours(0),
-        first_opposite,
-        lambda: second_neighbours(1),
-        lambda: second_opposite(0),
-        lambda: second_neighbours(2),
-        lambda: second_opposite(1),
-        lambda: second_neighbours(3),
-        lambda: second_opposite(2),
-        lambda: second_opposite(3),
-        lambda: from_core(0),
-        lambda: from_core(1),
+        lambda: start(0),
+        lambda: forward(0),
+        turn,
+        lambda: forward(1),
+        lambda: close(1),
+        from_core,
     ]
-
-
-def project_kernel(
-    h_ref,
-    kw_ref,
-    vw_ref,
-    gain_ref,
-    raw_ref,
-    gk_ref,
-    gv_ref,
-    w_ref,
-    load_sem,
-    send_sem,
-    recv_sem,
-):
-    x, z, core = place()
-    steps, tile, width = w_ref.shape[1:]
-
-    def load(kv, i):
-        src = (kw_ref, vw_ref)[kv].at[pl.ds(i * tile, tile)]
-        return pltpu.make_async_copy(src, w_ref.at[kv, i], load_sem.at[kv, i])
-
-    for i in range(steps):
-        for kv in range(2):
-            load(kv, i).start()
-    greet(plane_peers())
-    sums = [jnp.zeros((h_ref.shape[0], width), F32)] * 2
-    for i in range(steps):
-        part = h_ref[:, i * tile : (i + 1) * tile]
-        for kv in range(2):
-            load(kv, i).wait()
-            sums[kv] = sums[kv] + jnp.dot(part, w_ref[kv, i], preferred_element_type=F32)
-    raw_ref[...] = sums[0]
-    gv_ref[x, z, core] = sums[1].astype(BF16)
-    parts = []
-    for i in range(width // 128):
-        keys = sums[0][:, i * 128 : (i + 1) * 128]
-        inv = lax.rsqrt(jnp.mean(keys * keys, axis=1, keepdims=True) + NORM_EPS)
-        parts.append((keys * inv * gain_ref[...]).astype(BF16))
-    gk_ref[x, z, core] = jnp.concatenate(parts, axis=1)
-    copies = Copies(send_sem, recv_sem)
-    for stage in gather_stages((gk_ref, gv_ref), copies):
-        stage()
-    copies.finish()
-
-
-def project_and_gather(hidden, key_weight, value_weight, gain):
-    rows, depth = hidden.shape
-    width = key_weight.shape[1]
-    tile = 1024
-    steps = depth // tile
-    vmem, anywhere = pl.BlockSpec(memory_space=pltpu.VMEM), pl.BlockSpec(memory_space=pl.ANY)
-    plane = jax.ShapeDtypeStruct((SIDE, SIDE, 2, rows, width), BF16)
-    raw, keys, values = pl.pallas_call(
-        project_kernel,
-        out_shape=[jax.ShapeDtypeStruct((rows, width), F32), plane, plane],
-        in_specs=[vmem, anywhere, anywhere, vmem],
-        out_specs=[vmem] * 3,
-        scratch_shapes=[
-            pltpu.VMEM((2, steps, tile, width), BF16),
-            pltpu.SemaphoreType.DMA((2, steps)),
-            pltpu.SemaphoreType.DMA((GATHER_COPIES,)),
-            pltpu.SemaphoreType.DMA((GATHER_COPIES,)),
-        ],
-        compiler_params=params(60, collective_id=0, has_side_effects=True),
-        name="project_and_gather",
-    )(hidden, key_weight, value_weight, gain)
-    total = SIDE * SIDE * 2 * rows
-    return raw, keys.reshape(total, width), values.reshape(total, width)
 
 
 def slots_of(lengths_ref, ids):
@@ -288,47 +199,94 @@
     return jnp.where(ids == lax.broadcasted_iota(jnp.int32, (rows, responses), 1), 1.0, 0.0)
 
 
-def attend_kernel(
+WINDOW = 256
+
+
+def forward_kernel(
     scale,
+    hidden_ref,
+    kw_ref,
+    vw_ref,
+    gain_ref,
     q_ref,
     t_ref,
-    k_ref,
-    v_ref,
     r_ref,
     lengths_ref,
     h_ref,
-    e_ref,
+    raw_ref,
+    e_out,
     g_ref,
     inv_ref,
     dq_ref,
     tok_ref,
     o_ref,
+    w_ref,
+    kv_ref,
+    e_ref,
+    dot_ref,
+    load_sem,
+    gather_send,
+    gather_recv,
     own_sem,
-    send_sem,
-    recv_sem,
+    spread_send,
+    spread_recv,
+    e_sem,
 ):
+    x, z, core = place()
     me = lax.axis_index("ctx")
     n = o_ref.shape[0]
+    second_pass, head, part = (pl.program_id(i) for i in range(3))
+    kv_heads, steps = e_ref.shape[:2]
+    at_step = (second_pass * kv_heads + head) * steps + part
+    half = kv_heads * steps
+    rows, heads = q_ref.shape[0], q_ref.shape[1] // 128
+    prompt_rows = raw_ref.shape[0]
+    tokens = n * prompt_rows
+    factor = scale * LOG2E
+
+    def load(kv, i):
+        tile = w_ref.shape[2]
+        src = (kw_ref, vw_ref)[kv].at[pl.ds(i * tile, tile)]
+        return pltpu.make_async_copy(src, w_ref.at[kv, i], load_sem.at[kv, i])
+
+    gather_copies = Copies(gather_send, gather_recv)
+    per = kv_heads // 2
+    gathers = [
+        gather_stages(
+            lambda kv, i=i: kv_ref.at[kv, pl.ds(i, 1)],
+            prompt_rows,
+            gather_copies,
+            i * GATHER_COPIES,
+        )
+        for i in range(2)
+    ]
 
     def window(peer):
         tile = 5 * (peer // 4) + peer % 4
         return h_ref.at[:, pl.ds(pl.multiple_of(tile * 128, 128), WINDOW)]
 
-    def copy(k):
+    def spread(k):
         peer = (me + k) % n
         return pltpu.make_async_remote_copy(
             src_ref=window(peer),
             dst_ref=o_ref.at[me],
-            send_sem=send_sem.at[k - 1],
-            recv_sem=recv_sem.at[k - 1],
+            send_sem=spread_send.at[k - 1],
+            recv_sem=spread_recv.at[k - 1],
             device_id={"ctx": peer},
             device_id_type=MESH,
         )
 
     own_copy = pltpu.make_async_copy(window(me), o_ref.at[me], own_sem)
 
-    @pl.when((pl.program_id(0) == 0) & (pl.program_id(1) == 0))
+    def keep(i):
+        place_of = (i // steps, i % steps)
+        return pltpu.make_async_copy(e_ref.at[place_of], e_out.at[place_of], e_sem.at[i])
+
+    @pl.when(at_step == 0)
     def _():
+        for i in range(w_ref.shape[1]):
+            for kv in range(2):
+                load(kv, i).start()
         barrier = pltpu.get_barrier_semaphore()
 
         def hello(k, carry):
@@ -337,157 +295,232 @@
             )
             return carry
 
+        lax.fori_loop(1, n, hello, 0)
+        tile, width = w_ref.shape[2:]
+        sums = [jnp.zeros((prompt_rows, width), F32)] * 2
+        for i in range(w_ref.shape[1]):
+            piece = hidden_ref[:, i * tile : (i + 1) * tile]
+            for kv in range(2):
+                load(kv, i).wait()
+                sums[kv] = sums[kv] + jnp.dot(piece, w_ref[kv, i], preferred_element_type=F32)
+        raw_ref[...] = sums[0]
+        for i in range(kv_heads):
+            keys = sums[0][:, i * 128 : (i + 1) * 128]
+            inv = lax.rsqrt(jnp.mean(keys * keys, axis=1, keepdims=True) + NORM_EPS)
+            lanes = slice(i % per * 128, (i % per + 1) * 128)
+            kv_ref[0, i // per, x, z, core, :, lanes] = (keys * inv * gain_ref[...]).astype(BF16)
+            kv_ref[1, i // per, x, z, core, :, lanes] = sums[1][:, i * 128 : (i + 1) * 128].astype(BF16)
+        tok_ref[...] = jnp.zeros_like(tok_ref)
+        pl.semaphore_wait(barrier, n - 1)
+        now, later = gathers
+        for stage in (now[0], now[1], now[2], later[0], now[3], later[1], now[4], later[2], now[5]):
+            stage()
+
+    pad = -rows % 128
+    filler = jnp.zeros((pad, 128), BF16)
+
+    def gathered(kv):
+        lanes = pl.ds(pl.multiple_of(head % per * 128, 128), 128)
+        return kv_ref[kv, head // per, :, :, :, :, lanes].reshape(tokens, 128)
+
+    def keys_of():
+        k = gathered(0)
+        return k, jnp.concatenate([r_ref[0], filler], axis=0)
+
+    def values_of():
+        v = gathered(1)
+        return v, jnp.concatenate([r_ref[1], filler], axis=0)
+
+    def two(ref, i):
+        return jnp.concatenate(
+            [ref[:, i * 128 : (i + 1) * 128], ref[:, (i + 1) * 128 : (i + 2) * 128]], axis=0
+        )
+
+    def these(i):
+        return slice(i * rows, (i + 2) * rows)
+
+    pairs = range(0, heads, 2)
+
+    @pl.when(second_pass == 0)
+    def _():
+        (k, rk), (v, rv) = keys_of(), values_of()
+        bias = slot_bias(lengths_ref, rows, rows + pad)
+        bias = jnp.concatenate([bias, bias], axis=0)
+
+        def logits(i):
+            q = two(q_ref, i)
+            s = lax.dot_general(q, k, NT, preferred_element_type=F32)
+            return s, lax.dot_general(q, rk, NT, preferred_element_type=F32) + bias
+
+        def weigh(i, s, sr):
+            peak = jnp.maximum(
+                jnp.max(s, axis=1, keepdims=True), jnp.max(sr, axis=1, keepdims=True)
+            )
+            top = peak * factor
+            e = jnp.exp2(s * factor - top)
+            er = jnp.exp2(sr * factor - top)
+            inv = 1.0 / (
+                jnp.sum(e, axis=1, keepdims=True) + jnp.sum(er, axis=1, keepdims=True)
+            )
+            e_ref[head, part, these(i), :tokens] = e.astype(BF16)
+            e_ref[head, part, these(i), tokens:] = er.astype(BF16)
+            inv_ref[head, part, these(i)] = inv
+            return inv
+
+        def read(i, inv):
+            t = two(t_ref, i)
+            e = e_ref[head, part, these(i), :tokens]
+            er = e_ref[head, part, these(i), tokens:]
+            attended = jnp.dot(e, v, preferred_element_type=F32)
+            attended = (attended + jnp.dot(er, rv, preferred_element_type=F32)) * inv
+            dot = jnp.sum(attended * t.astype(F32), axis=1, keepdims=True)
+            dot_ref[head, part, these(i)] = dot
+            return dot[:rows] + dot[rows:]
+
+        scores = {i: logits(i) for i in pairs}
+        total = jnp.zeros((rows, 1), F32)
+        for i in pairs:
+            total = total + read(i, weigh(i, *scores[i]))
+        tok_ref[...] += total
+        keep(at_step).start()
+
+    @pl.when(second_pass == 1)
+    def _():
+        (k, rk), (v, rv) = keys_of(), values_of()
+
+        def products(i):
+            t = two(t_ref, i)
+            return (
+                lax.dot_general(t, v, NT, preferred_element_type=F32),
+                lax.dot_general(t, rv, NT, preferred_element_type=F32),
+            )
+
+        def differ(i, dp, dpr):
+            dot = dot_ref[head, part, these(i)]
+            e = e_ref[head, part, these(i), :tokens]
+            er = e_ref[head, part, these(i), tokens:]
+            g_ref[0, 0, these(i), :tokens] = (e.astype(F32) * (dp - dot)).astype(BF16)
+            g_ref[0, 0, these(i), tokens:] = (er.astype(F32) * (dpr - dot)).astype(BF16)
+
+        def query_grad(i):
+            g, gr = g_ref[0, 0, these(i), :tokens], g_ref[0, 0, these(i), tokens:]
+            dq = jnp.dot(g, k, preferred_element_type=F32)
+            dq = dq + jnp.dot(gr, rk, preferred_element_type=F32)
+            dq = dq * (inv_ref[head, part, these(i)] * scale)
+            dq_ref[:, i * 128 : (i + 1) * 128] = dq[:rows].astype(BF16)
+            dq_ref[:, (i + 1) * 128 : (i + 2) * 128] = dq[rows:].astype(BF16)
+
+        dps = {i: products(i) for i in pairs}
+        for i in pairs:
+            differ(i, *dps[i])
+            query_grad(i)
+
+    def after(step, work):
+        pl.when(at_step == step)(work)
+
+    def hidden_columns():
         def go(k, carry):
-            copy(k).start()
+            spread(k).start()
             return carry
 
-        lax.fori_loop(1, n, hello, 0)
-        pl.semaphore_wait(barrier, n - 1)
         lax.fori_loop(1, n, go, 0)
         own_copy.start()
-        tok_ref[...] = jnp.zeros_like(tok_ref)
-
-    rows, heads = q_ref.shape[0], q_ref.shape[1] // 128
-    tokens = k_ref.shape[0]
-    pad = -rows % 128
-    filler = jnp.zeros((pad, 128), BF16)
-    k, v = k_ref[...], v_ref[...]
-    rk = jnp.concatenate([r_ref[0], filler], axis=0)
-    rv = jnp.concatenate([r_ref[1], filler], axis=0)
-    bias = slot_bias(lengths_ref, rows, rows + pad)
-    factor = scale * LOG2E
-    parts = range(0, heads, 2)
-    bias = jnp.concatenate([bias, bias], axis=0)
-
-    def two(ref, i):
-        return jnp.concatenate([ref[:, i * 128 : (i + 1) * 128], ref[:, (i + 1) * 128 : (i + 2) * 128]], axis=0)
-
-    def out_rows(i):
-        return slice(i * rows, (i + 2) * rows)
-
-    def logits(i):
-        q = two(q_ref, i)
-        s = lax.dot_general(q, k, NT, preferred_element_type=F32)
-        return s, lax.dot_general(q, rk, NT, preferred_element_type=F32) + bias
-
-    def weigh(i, s, sr):
-        peak = jnp.maximum(
-            jnp.max(s, axis=1, keepdims=True), jnp.max(sr, axis=1, keepdims=True)
-        )
-        top = peak * factor
-        e = jnp.exp2(s * factor - top)
-        er = jnp.exp2(sr * factor - top)
-        inv = 1.0 / (
-            jnp.sum(e, axis=1, keepdims=True) + jnp.sum(er, axis=1, keepdims=True)
-        )
-        e_ref[0, out_rows(i), :tokens] = e.astype(BF16)
-        e_ref[0, out_rows(i), tokens:] = er.astype(BF16)
-        inv_ref[0, out_rows(i)] = inv
-        return inv
-
-    def read(i, inv):
-        t = two(t_ref, i)
-        e, er = e_ref[0, out_rows(i), :tokens], e_ref[0, out_rows(i), tokens:]
-        dp = lax.dot_general(t, v, NT, preferred_element_type=F32)
-        dpr = lax.dot_general(t, rv, NT, preferred_element_type=F32)
-        attended = jnp.dot(e, v, preferred_element_type=F32)
-        attended = (attended + jnp.dot(er, rv, preferred_element_type=F32)) * inv
-        dot = jnp.sum(attended * t.astype(F32), axis=1, keepdims=True)
-        return dp, dpr, dot
-
-    def differ(i, dp, dpr, dot):
-        e, er = e_ref[0, out_rows(i), :tokens], e_ref[0, out_rows(i), tokens:]
-        g_ref[0, out_rows(i), :tokens] = (e.astype(F32) * (dp - dot)).astype(BF16)
-        g_ref[0, out_rows(i), tokens:] = (er.astype(F32) * (dpr - dot)).astype(BF16)
-
-    def query_grad(i, inv):
-        g, gr = g_ref[0, out_rows(i), :tokens], g_ref[0, out_rows(i), tokens:]
-        dq = jnp.dot(g, k, preferred_element_type=F32)
-        dq = (dq + jnp.dot(gr, rk, preferred_element_type=F32)) * (inv * scale)
-        dq_ref[:, i * 128 : (i + 1) * 128] = dq[:rows].astype(BF16)
-        dq_ref[:, (i + 1) * 128 : (i + 2) * 128] = dq[rows:].astype(BF16)
-
-    scores = {i: logits(i) for i in parts}
-    invs, reads, total = {}, {}, jnp.zeros((rows, 1), F32)
-    for i in parts:
-        invs[i] = weigh(i, *scores[i])
-        reads[i] = read(i, invs[i])
-        if i >= 2:
-            differ(i - 2, *reads[i - 2])
-            query_grad(i - 2, invs[i - 2])
-    last = heads - 2
-    differ(last, *reads[last])
-    query_grad(last, invs[last])
-    for i in parts:
-        dot = reads[i][2]
-        total = total + dot[:rows] + dot[rows:]
-    tok_ref[...] += total
-
-    @pl.when(
-        (pl.program_id(0) == pl.num_programs(0) - 1) & (pl.program_id(1) == pl.num_programs(1) - 1)
-    )
-    def _():
+
+    def last():
+        for i in range(half):
+            keep(i).wait()
+        own_copy.wait()
+
         def done(k, carry):
-            copy(k).wait()
+            spread(k).wait()
             return carry
 
-        own_copy.wait()
         lax.fori_loop(1, n, done, 0)
-
-
-WINDOW = 256
-
-
-def attend(q, t, prompt_keys, prompt_values, resp, lengths, hidden, n, scale, grouped, chunk):
-    rows = q.shape[0]
-    tokens, kv_width = prompt_keys.shape
+        gather_copies.draining = True
+        for gather in gathers:
+            for stage in gather:
+                stage()
+
+    after(0, gathers[1][3])
+    after(1, gathers[1][4])
+    after(half // 2 - 1, gathers[1][5])
+    after(half // 2, hidden_columns)
+    after(2 * half - 1, last)
+
+
+def forward(
+    hidden, kw, vw, gain, q, t, resp, lengths, n, scale, grouped, chunk
+):
+    rows, depth = q.shape[0], hidden.shape[1]
+    prompt_rows, kv_width = hidden.shape[0], kw.shape[1]
     kv_heads = kv_width // 128
-    pad = rows + -rows % 128
+    width = n * prompt_rows + rows + -rows % 128
     steps = grouped // chunk
     m = chunk * rows
-    total = grouped * rows
-    row_block = pl.BlockSpec((rows, chunk * 128), lambda h, c: (0, h * steps + c))
-    head_block = pl.BlockSpec((tokens, 128), lambda h, c: (0, h))
-
-    def score_block(width):
-        return pl.BlockSpec((1, m, width), lambda h, c: (h, c, 0))
-
+    tile = 1024
+    last = kv_heads * steps - 1
+    dma = pltpu.SemaphoreType.DMA
+    smem, anywhere = pl.BlockSpec(memory_space=pltpu.SMEM), pl.BlockSpec(memory_space=pl.ANY)
+
+    def whole(*shape):
+        return pl.BlockSpec(shape, lambda p, h, c: (0,) * len(shape))
+
+    def step_of(h, c):
+        return h * steps + c
+
+    first_only = pl.BlockSpec(
+        (rows, chunk * 128), lambda p, h, c: (0, step_of(h, c) * (1 - p) + last * p)
+    )
+    both = pl.BlockSpec((rows, chunk * 128), lambda p, h, c: (0, step_of(h, c)))
+    second_only = pl.BlockSpec((rows, chunk * 128), lambda p, h, c: (0, step_of(h, c) * p))
     return pl.pallas_call(
-        functools.partial(attend_kernel, scale),
-        grid=(kv_heads, steps),
+        functools.partial(forward_kernel, scale),
+        grid=(2, kv_heads, steps),
         in_specs=[
-            row_block,
-            row_block,
-            head_block,
-            head_block,
-            pl.BlockSpec((2, rows, 128), lambda h, c: (0, 0, h)),
-            pl.BlockSpec(memory_space=pltpu.SMEM),
-            pl.BlockSpec(memory_space=pl.ANY),
+            whole(prompt_rows, depth),
+            anywhere,
+            anywhere,
+            whole(1, 128),
+            first_only,
+            both,
+            pl.BlockSpec((2, rows, 128), lambda p, h, c: (0, 0, h)),
+            smem,
+            anywhere,
         ],
         out_specs=[
-            score_block(tokens + pad),
-            score_block(tokens + pad),
-            score_block(1),
-            row_block,
-            pl.BlockSpec((rows, 1), lambda h, c: (0, 0)),
-            pl.BlockSpec(memory_space=pl.ANY),
+            whole(prompt_rows, kv_width),
+            anywhere,
+            pl.BlockSpec((1, 1, m, width), lambda p, h, c: (h * p, c * p, 0, 0)),
+            whole(kv_heads, steps, m, 1),
+            second_only,
+            whole(rows, 1),
+            anywhere,
         ],
         out_shape=[
-            jax.ShapeDtypeStruct((kv_heads, total, tokens + pad), BF16),
-            jax.ShapeDtypeStruct((kv_heads, total, tokens + pad), BF16),
-            jax.ShapeDtypeStruct((kv_heads, total, 1), F32),
+            jax.ShapeDtypeStruct((prompt_rows, kv_width), F32),
+            jax.ShapeDtypeStruct((kv_heads, steps, m, width), BF16),
+            jax.ShapeDtypeStruct((kv_heads, steps, m, width), BF16),
+            jax.ShapeDtypeStruct((kv_heads, steps, m, 1), F32),
             jax.ShapeDtypeStruct(q.shape, BF16),
             jax.ShapeDtypeStruct((rows, 1), F32),
-            jax.ShapeDtypeStruct((n, hidden.shape[0], WINDOW), BF16),
+            jax.ShapeDtypeStruct((n, prompt_rows, WINDOW), BF16),
         ],
         scratch_shapes=[
-            pltpu.SemaphoreType.DMA,
-            pltpu.SemaphoreType.DMA((n - 1,)),
-            pltpu.SemaphoreType.DMA((n - 1,)),
+            pltpu.VMEM((2, depth // tile, tile, kv_width), BF16),
+            pltpu.VMEM((2, 2, SIDE, SIDE, 2, prompt_rows, kv_width // 2), BF16),
+            pltpu.VMEM((kv_heads, steps, m, width), BF16),
+            pltpu.VMEM((kv_heads, steps, m, 1), F32),
+            dma((2, depth // tile)),
+            dma((2 * GATHER_COPIES,)),
+            dma((2 * GATHER_COPIES,)),
+            dma,
+            dma((n - 1,)),
+            dma((n - 1,)),
+            dma((kv_heads * steps,)),
         ],
-        compiler_params=params(56, collective_id=3, has_side_effects=True),
-        name="attend",
-    )(q, t, prompt_keys, prompt_values, resp, lengths, hidden)
+        compiler_params=params(60, collective_id=0, has_side_effects=True),
+        name="forward",
+    )(hidden, kw, vw, gain, q, t, resp, lengths, hidden)
 
 
 def norm_backward(raw, gain, grad):
@@ -784,9 +817,9 @@
         for h in range(kv_heads):
             grads = lax.dot_general(rbuf_ref[kv, h], scaled[h], TN, preferred_element_type=F32)
             resp_ref[kv, :, h * 128 : (h + 1) * 128] = grads[:rows].astype(BF16)
-    qgrad_ref[...] = (dq_ref[...].astype(F32) * row_grad).astype(BF16)
     loss = jnp.maximum(-margin, 0.0) + jnp.log1p(small)
     loss_ref[...] = jnp.sum(loss, axis=1, keepdims=True)
+    qgrad_ref[...] = (dq_ref[...].astype(F32) * row_grad).astype(BF16)
     for kv in range(2):
         reduce.end_inner(kv, 2)
     for kv in range(2):
@@ -794,11 +827,13 @@
     for kv in range(2):
         reduce.end_inner(kv, 3)
     key_sum = reduce.result(0, None)
-    gk_ref[x, z, core] = norm_backward(raw_ref[...], gain_ref[...], key_sum).astype(BF16)
-    gv_ref[x, z, core] = reduce.result(1, None).astype(BF16)
+    gk_ref[0, x, z, core] = norm_backward(raw_ref[...], gain_ref[...], key_sum).astype(BF16)
+    gv_ref[0, x, z, core] = reduce.result(1, None).astype(BF16)
 
     gather_copies = Copies(gather_send, gather_recv)
-    stages = gather_stages((gk_ref, gv_ref), gather_copies)
+    stages = gather_stages(
+        lambda kv: (gk_ref, gv_ref)[kv], raw_ref.shape[0], gather_copies, 0
+    )
     last_copies = Copies(last_send, last_recv)
     stages[0]()
     wait(late)
@@ -806,7 +841,7 @@
     half = paway_ref.shape[1]
 
     def input_grad(side, store):
-        key_grad, value_grad = gk_ref[x, z, core], gv_ref[x, z, core]
+        key_grad, value_grad = gk_ref[0, x, z, core], gv_ref[0, x, z, core]
 
         def step(i, carry):
             here = pl.ds(pl.multiple_of(side * half + i * tile, tile), tile)
@@ -825,20 +860,20 @@
 
     input_grad(1 - tp, store_away)
     last_copies.send(paway_ref, pcame_ref, {"tp": 1 - tp}, 0)
-    for stage in stages[1:5]:
-        stage()
+    stages[1]()
+    stages[2]()
     input_grad(tp, store_own)
-    for stage in stages[5:-2]:
-        stage()
+    stages[3]()
+    stages[4]()
     last_copies.arrived(pcame_ref, 0)
     pgrad_ref[...] = (pown_ref[...] + pcame_ref[...].astype(F32)).astype(BF16)
 
     out_rows = wgrad_ref.shape[0]
     shift = (ctx % 4) * 32
     hidden = h_ref[...].reshape(-1, h_ref.shape[2])
+    stages[5]()
     for kv, ref in enumerate((gk_ref, gv_ref)):
-        stages[-2 + kv]()
-        grads = ref[...].reshape(-1, ref.shape[4])
+        grads = ref[...].reshape(-1, ref.shape[5])
         wpart_ref[kv] = lax.dot_general(hidden, grads, TN, preferred_element_type=F32)
         away = pl.ds(pl.multiple_of(shift + (1 - dp) * out_rows, 16), out_rows)
         waway_ref[kv] = wpart_ref[kv, away].astype(BF16)
@@ -909,8 +944,8 @@
             pltpu.VMEM((2, SIDE, 6) + small, BF16),
             pltpu.VMEM((2, SIDE, prompt_rows, kv_width), BF16),
             pltpu.VMEM((2, 6) + small, BF16),
-            pltpu.VMEM((SIDE, SIDE, 2, prompt_rows, kv_width), BF16),
-            pltpu.VMEM((SIDE, SIDE, 2, prompt_rows, kv_width), BF16),
+            pltpu.VMEM((1, SIDE, SIDE, 2, prompt_rows, kv_width), BF16),
+            pltpu.VMEM((1, SIDE, SIDE, 2, prompt_rows, kv_width), BF16),
             pltpu.VMEM((2, depth, kv_width), BF16),
             pltpu.VMEM(windows.shape, BF16),
             pltpu.VMEM((prompt_rows, half), BF16),
@@ -950,6 +985,30 @@
     )
 
 
+def finish_kernel(*refs):
+    count = len(refs) // 2
+    copies = [
+        pltpu.make_async_copy(refs[i], refs[count + i], refs[-1].at[i]) for i in range(count)
+    ]
+    for one in copies:
+        one.start()
+    for one in copies:
+        one.wait()
+
+
+def finish(*arrays):
+    anywhere = pl.BlockSpec(memory_space=pl.ANY)
+    return pl.pallas_call(
+        finish_kernel,
+        out_shape=[jax.ShapeDtypeStruct(a.shape, a.dtype) for a in arrays],
+        in_specs=[anywhere] * len(arrays),
+        out_specs=[anywhere] * len(arrays),
+        scratch_shapes=[pltpu.SemaphoreType.DMA((len(arrays),))],
+        compiler_params=params(16),
+        name="finish",
+    )(*arrays)
+
+
 def shards(
     prompt_hidden,
     key_weight,
@@ -963,35 +1022,32 @@
     placement_map,
 ):
     hidden = prompt_hidden[0]
-    prompt_rows, model_width = hidden.shape
+    model_width = hidden.shape[1]
     head_width = key_gain.shape[0]
     kv_width = key_weight.shape[1]
-    kv_heads = kv_width // head_width
-    query_heads = queries.shape[2] // head_width
-    grouped = query_heads // kv_heads
+    grouped = queries.shape[2] // kv_width
     n_ctx = lax.axis_size("ctx")
     qk_scale = 1.0 / math.sqrt(head_width)
     gain = key_gain[None]
-
-    raw_keys, prompt_keys, prompt_values = project_and_gather(
-        hidden, key_weight, value_weight, gain
-    )
-
-    resp = response_kv[0].transpose(1, 0, 2)
     q, t = queries[0], targets[0]
-    e, g, inv, dq, token_part, windows = attend(
+    raw_keys, e, g, inv, dq, token_part, windows = forward(
+        hidden,
+        key_weight,
+        value_weight,
+        gain,
         q,
         t,
-        prompt_keys,
-        prompt_values,
-        resp,
+        response_kv[0].transpose(1, 0, 2),
         lengths[0, 0],
-        hidden,
         n_ctx,
         qk_scale,
         grouped,
         4,
     )
+
+    def joined(value):
+        return value.reshape(value.shape[0], -1, value.shape[3])
+
     dpo_loss, query_grad, resp_grad, prompt_grad, weight_grad = backward(
         token_part,
         lengths[0, 0],
@@ -999,18 +1055,19 @@
         ref_scores,
         q,
         t,
-        inv,
+        joined(inv),
         dq,
         raw_keys,
         gain,
-        e,
-        g,
+        joined(e),
+        joined(g),
         key_weight,
         value_weight,
         windows,
         qk_scale,
         model_width // n_ctx // 2,
     )
+    query_grad, prompt_grad, weight_grad = finish(query_grad, prompt_grad, weight_grad)
     return (
         dpo_loss.reshape(1),
         query_grad[None],

time: 138 us -> 139 us (level)
  Pallas kernels: 126 us -> 130 us
  local copies, waits for them, and re-layouts: 8.93 us -> 6.5 us
    pallas_call x1, Pallas kernels: 66.1 us -> 69.3 us  [backward(): pl.pallas_call(functools.partial(backward_kernel, scale), out_shape=[jax....]
    unnamed x5 -> x8, local copies, waits for them, and re-layouts: 8.93 us -> 6.5 us
where the time goes in v4:
time: 139 us
  Pallas kernels  130 us (94%)
  local copies, waits for them, and re-layouts  6.5 us (5%)
  between operations  2.42 us (2%)
    pallas_call x1, Pallas kernels, backward(): pl.pallas_call(functools.partial(backward_kernel, scale), out_shape=[jax....  69.3 us
    pallas_call x1, Pallas kernels, forward(): pl.pallas_call(functools.partial(forward_kernel, scale), grid=(2, kv_head...  59.6 us
    unnamed x8, local copies, waits for them, and re-layouts  6.5 us

profile of v4, /device:TPU:1, one launch (start us, length us, event | category | flops | bytes accessed | tf_op | source)
XLA Modules:
  0.0 139.0 jit_solution(7419680750184999088)
XLA Ops:
  0.6 1.6 %copy.18 = bf16[1,96,2,512]{3,1,2,0:T(8,128)(2,1)} copy(bf16[1,96,2,512]{3,2,1,0:T(2,128)(2,1)} %param.15) | data formatting | bytes 393216 | tf_op args[5]
  2.3 59.6 %forward.1 = (f32[64,512]{1,0:T(8,128)}, bf16[4,2,384,2176]{3,2,1,0:T(8,128)(2,1)}, bf16[4,2,384,2176]{3,2,1,0:T(8,128)(2,1)}, f32[4,2,384,1]{3,2,1,0:T(8,128)},...) custom-call(bf16[64,5120]{1,0:T(8,128)(2,1)} %bitcast.26, bf16[5120,512]{1,0:T(8,128)(2,1)} %kw_ref.3, ...), custom_call_target="tpu_custom_call" | custom-call | tf_op jit(solution)/shard_map/forward/pallas_call | solution.py:476
  61.9 69.3 %backward.1 = (f32[1,1]{1,0:T(1,128)}, bf16[96,4096]{1,0:T(8,128)(2,1)}, bf16[2,96,512]{2,1,0:T(8,128)(2,1)}, bf16[64,2560]{1,0:T(8,128)(2,1)}, f32[80,2,512]{2,1,0:T(2,128)}) custom-call(f32[96,1]{1,0:T(8,128)} %get-tuple-element.20.token_ref, s32[8]{0:T(128)} %bitcast.34, s32[8]{0:T(128)} %bitcast.35, f32[1,256]{1,0:T(1,128)} %ref_ref.1, ...), custom_call_target="tpu_custom_call" | custom-call | tf_op jit(solution)/shard_map/backward/pallas_call | solution.py:922
  131.2 0.0 copy-start
  131.2 1.1 copy-done
  132.3 0.0 copy-start.1
  132.3 1.0 copy-done.1
  133.3 0.0 copy-start.2
  133.3 1.0 copy-done.2
  134.3 1.1 finish.1
  135.4 1.8 %copy.16 = bf16[1,96,2,512]{3,2,1,0:T(2,128)(2,1)} copy(bf16[1,96,2,512]{3,1,2,0:T(8,128)(2,1)} %bitcast.30) | data formatting | bytes 393216
Async XLA Ops:
  131.2 1.1 copy-start
  132.3 1.0 copy-start.1
  133.3 1.0 copy-start.2

commit v5 on v4

--- a/solution.py
+++ b/solution.py
@@ -214,7 +214,7 @@
     lengths_ref,
     h_ref,
     raw_ref,
-    e_out,
+    e_ref,
     g_ref,
     inv_ref,
     dq_ref,
@@ -222,23 +222,20 @@
     o_ref,
     w_ref,
     kv_ref,
-    e_ref,
-    dot_ref,
     load_sem,
     gather_send,
     gather_recv,
     own_sem,
     spread_send,
     spread_recv,
-    e_sem,
 ):
     x, z, core = place()
     me = lax.axis_index("ctx")
     n = o_ref.shape[0]
-    second_pass, head, part = (pl.program_id(i) for i in range(3))
-    kv_heads, steps = e_ref.shape[:2]
-    at_step = (second_pass * kv_heads + head) * steps + part
-    half = kv_heads * steps
+    head, part = pl.program_id(0), pl.program_id(1)
+    kv_heads, steps = inv_ref.shape[:2]
+    at_step = head * steps + part
+    half = kv_heads * steps // 2
     rows, heads = q_ref.shape[0], q_ref.shape[1] // 128
     prompt_rows = raw_ref.shape[0]
     tokens = n * prompt_rows
@@ -277,10 +274,6 @@
         )
 
     own_copy = pltpu.make_async_copy(window(me), o_ref.at[me], own_sem)
-
-    def keep(i):
-        place_of = (i // steps, i % steps)
-        return pltpu.make_async_copy(e_ref.at[place_of], e_out.at[place_of], e_sem.at[i])
 
     @pl.when(at_step == 0)
     def _():
@@ -340,80 +333,65 @@
         return slice(i * rows, (i + 2) * rows)
 
     pairs = range(0, heads, 2)
-
-    @pl.when(second_pass == 0)
-    def _():
-        (k, rk), (v, rv) = keys_of(), values_of()
-        bias = slot_bias(lengths_ref, rows, rows + pad)
-        bias = jnp.concatenate([bias, bias], axis=0)
-
-        def logits(i):
-            q = two(q_ref, i)
-            s = lax.dot_general(q, k, NT, preferred_element_type=F32)
-            return s, lax.dot_general(q, rk, NT, preferred_element_type=F32) + bias
-
-        def weigh(i, s, sr):
-            peak = jnp.maximum(
-                jnp.max(s, axis=1, keepdims=True), jnp.max(sr, axis=1, keepdims=True)
-            )
-            top = peak * factor
-            e = jnp.exp2(s * factor - top)
-            er = jnp.exp2(sr * factor - top)
-            inv = 1.0 / (
-                jnp.sum(e, axis=1, keepdims=True) + jnp.sum(er, axis=1, keepdims=True)
-            )
-            e_ref[head, part, these(i), :tokens] = e.astype(BF16)
-            e_ref[head, part, these(i), tokens:] = er.astype(BF16)
-            inv_ref[head, part, these(i)] = inv
-            return inv
-
-        def read(i, inv):
-            t = two(t_ref, i)
-            e = e_ref[head, part, these(i), :tokens]
-            er = e_ref[head, part, these(i), tokens:]
-            attended = jnp.dot(e, v, preferred_element_type=F32)
-            attended = (attended + jnp.dot(er, rv, preferred_element_type=F32)) * inv
-            dot = jnp.sum(attended * t.astype(F32), axis=1, keepdims=True)
-            dot_ref[head, part, these(i)] = dot
-            return dot[:rows] + dot[rows:]
-
-        scores = {i: logits(i) for i in pairs}
-        total = jnp.zeros((rows, 1), F32)
-        for i in pairs:
-            total = total + read(i, weigh(i, *scores[i]))
-        tok_ref[...] += total
-        keep(at_step).start()
-
-    @pl.when(second_pass == 1)
-    def _():
-        (k, rk), (v, rv) = keys_of(), values_of()
-
-        def products(i):
-            t = two(t_ref, i)
-            return (
-                lax.dot_general(t, v, NT, preferred_element_type=F32),
-                lax.dot_general(t, rv, NT, preferred_element_type=F32),
-            )
-
-        def differ(i, dp, dpr):
-            dot = dot_ref[head, part, these(i)]
-            e = e_ref[head, part, these(i), :tokens]
-            er = e_ref[head, part, these(i), tokens:]
-            g_ref[0, 0, these(i), :tokens] = (e.astype(F32) * (dp - dot)).astype(BF16)
-            g_ref[0, 0, these(i), tokens:] = (er.astype(F32) * (dpr - dot)).astype(BF16)
-
-        def query_grad(i):
-            g, gr = g_ref[0, 0, these(i), :tokens], g_ref[0, 0, these(i), tokens:]
-            dq = jnp.dot(g, k, preferred_element_type=F32)
-            dq = dq + jnp.dot(gr, rk, preferred_element_type=F32)
-            dq = dq * (inv_ref[head, part, these(i)] * scale)
-            dq_ref[:, i * 128 : (i + 1) * 128] = dq[:rows].astype(BF16)
-            dq_ref[:, (i + 1) * 128 : (i + 2) * 128] = dq[rows:].astype(BF16)
-
-        dps = {i: products(i) for i in pairs}
-        for i in pairs:
-            differ(i, *dps[i])
-            query_grad(i)
+    (k, rk), (v, rv) = keys_of(), values_of()
+    bias = slot_bias(lengths_ref, rows, rows + pad)
+    bias = jnp.concatenate([bias, bias], axis=0)
+
+    def logits(i):
+        q = two(q_ref, i)
+        s = lax.dot_general(q, k, NT, preferred_element_type=F32)
+        return s, lax.dot_general(q, rk, NT, preferred_element_type=F32) + bias
+
+    def weigh(i, s, sr):
+        peak = jnp.maximum(
+            jnp.max(s, axis=1, keepdims=True), jnp.max(sr, axis=1, keepdims=True)
+        )
+        top = peak * factor
+        e = jnp.exp2(s * factor - top)
+        er = jnp.exp2(sr * factor - top)
+        inv = 1.0 / (jnp.sum(e, axis=1, keepdims=True) + jnp.sum(er, axis=1, keepdims=True))
+        e_ref[0, 0, these(i), :tokens] = e.astype(BF16)
+        e_ref[0, 0, these(i), tokens:] = er.astype(BF16)
+        inv_ref[head, part, these(i)] = inv
+        return inv
+
+    def read(i, inv):
+        t = two(t_ref, i)
+        e, er = e_ref[0, 0, these(i), :tokens], e_ref[0, 0, these(i), tokens:]
+        dp = lax.dot_general(t, v, NT, preferred_element_type=F32)
+        dpr = lax.dot_general(t, rv, NT, preferred_element_type=F32)
+        attended = jnp.dot(e, v, preferred_element_type=F32)
+        attended = (attended + jnp.dot(er, rv, preferred_element_type=F32)) * inv
+        dot = jnp.sum(attended * t.astype(F32), axis=1, keepdims=True)
+        return dp, dpr, dot
+
+    def differ(i, dp, dpr, dot):
+        e, er = e_ref[0, 0, these(i), :tokens], e_ref[0, 0, these(i), tokens:]
+        g_ref[0, 0, these(i), :tokens] = (e.astype(F32) * (dp - dot)).astype(BF16)
+        g_ref[0, 0, these(i), tokens:] = (er.astype(F32) * (dpr - dot)).astype(BF16)
+
+    def query_grad(i, inv):
+        g, gr = g_ref[0, 0, these(i), :tokens], g_ref[0, 0, these(i), tokens:]
+        dq = jnp.dot(g, k, preferred_element_type=F32)
+        dq = (dq + jnp.dot(gr, rk, preferred_element_type=F32)) * (inv * scale)
+        dq_ref[:, i * 128 : (i + 1) * 128] = dq[:rows].astype(BF16)
+        dq_ref[:, (i + 1) * 128 : (i + 2) * 128] = dq[rows:].astype(BF16)
+
+    scores = {i: logits(i) for i in pairs}
+    invs, reads, total = {}, {}, jnp.zeros((rows, 1), F32)
+    for i in pairs:
+        invs[i] = weigh(i, *scores[i])
+        reads[i] = read(i, invs[i])
+        if i >= 2:
+            differ(i - 2, *reads[i - 2])
+            query_grad(i - 2, invs[i - 2])
+    final = heads - 2
+    differ(final, *reads[final])
+    query_grad(final, invs[final])
+    for i in pairs:
+        dot = reads[i][2]
+        total = total + dot[:rows] + dot[rows:]
+    tok_ref[...] += total
 
     def after(step, work):
         pl.when(at_step == step)(work)
@@ -427,8 +405,6 @@
         own_copy.start()
 
     def last():
-        for i in range(half):
-            keep(i).wait()
         own_copy.wait()
 
         def done(k, carry):
@@ -443,8 +419,8 @@
 
     after(0, gathers[1][3])
     after(1, gathers[1][4])
-    after(half // 2 - 1, gathers[1][5])
-    after(half // 2, hidden_columns)
+    after(half - 2, gathers[1][5])
+    after(half - 1, hidden_columns)
     after(2 * half - 1, last)
 
 
@@ -458,41 +434,34 @@
     steps = grouped // chunk
     m = chunk * rows
     tile = 1024
-    last = kv_heads * steps - 1
     dma = pltpu.SemaphoreType.DMA
     smem, anywhere = pl.BlockSpec(memory_space=pltpu.SMEM), pl.BlockSpec(memory_space=pl.ANY)
 
     def whole(*shape):
-        return pl.BlockSpec(shape, lambda p, h, c: (0,) * len(shape))
-
-    def step_of(h, c):
-        return h * steps + c
-
-    first_only = pl.BlockSpec(
-        (rows, chunk * 128), lambda p, h, c: (0, step_of(h, c) * (1 - p) + last * p)
-    )
-    both = pl.BlockSpec((rows, chunk * 128), lambda p, h, c: (0, step_of(h, c)))
-    second_only = pl.BlockSpec((rows, chunk * 128), lambda p, h, c: (0, step_of(h, c) * p))
+        return pl.BlockSpec(shape, lambda h, c: (0,) * len(shape))
+
+    row_block = pl.BlockSpec((rows, chunk * 128), lambda h, c: (0, h * steps + c))
+    kept_block = pl.BlockSpec((1, 1, m, width), lambda h, c: (h, c, 0, 0))
     return pl.pallas_call(
         functools.partial(forward_kernel, scale),
-        grid=(2, kv_heads, steps),
+        grid=(kv_heads, steps),
         in_specs=[
             whole(prompt_rows, depth),
             anywhere,
             anywhere,
             whole(1, 128),
-            first_only,
-            both,
-            pl.BlockSpec((2, rows, 128), lambda p, h, c: (0, 0, h)),
+            row_block,
+            row_block,
+            pl.BlockSpec((2, rows, 128), lambda h, c: (0, 0, h)),
             smem,
             anywhere,
         ],
         out_specs=[
             whole(prompt_rows, kv_width),
-            anywhere,
-            pl.BlockSpec((1, 1, m, width), lambda p, h, c: (h * p, c * p, 0, 0)),
+            kept_block,
+            kept_block,
             whole(kv_heads, steps, m, 1),
-            second_only,
+            row_block,
             whole(rows, 1),
             anywhere,
         ],
@@ -508,15 +477,12 @@
         scratch_shapes=[
             pltpu.VMEM((2, depth // tile, tile, kv_width), BF16),
             pltpu.VMEM((2, 2, SIDE, SIDE, 2, prompt_rows, kv_width // 2), BF16),
-            pltpu.VMEM((kv_heads, steps, m, width), BF16),
-            pltpu.VMEM((kv_heads, steps, m, 1), F32),
             dma((2, depth // tile)),
             dma((2 * GATHER_COPIES,)),
             dma((2 * GATHER_COPIES,)),
             dma,
             dma((n - 1,)),
             dma((n - 1,)),
-            dma((kv_heads * steps,)),
         ],
         compiler_params=params(60, collective_id=0, has_side_effects=True),
         name="forward",
@@ -1004,7 +970,7 @@
         in_specs=[anywhere] * len(arrays),
         out_specs=[anywhere] * len(arrays),
         scratch_shapes=[pltpu.SemaphoreType.DMA((len(arrays),))],
-        compiler_params=params(16),
+        compiler_params=params(61),
         name="finish",
     )(*arrays)
 

time: 139 us -> 178 us (1.28)
  Pallas kernels: 130 us -> 172 us
  local copies, waits for them, and re-layouts: 6.5 us -> 3.43 us
    pallas_call x1, Pallas kernels: 1.11 us -> 44.8 us  [finish(): pl.pallas_call(finish_kernel, out_shape=[jax.ShapeDtypeStruct(a.shape, a....]
    unnamed x8 -> x2, local copies, waits for them, and re-layouts: 6.5 us -> 3.43 us
    pallas_call x1, Pallas kernels: 59.6 us -> 57.4 us  [forward(): pl.pallas_call(functools.partial(forward_kernel, scale), grid=(kv_heads,...]
where the time goes in v5:
time: 178 us
  Pallas kernels  172 us (97%)
  local copies, waits for them, and re-layouts  3.43 us (2%)
  between operations  2.35 us (1%)
    pallas_call x1, Pallas kernels, backward(): pl.pallas_call(functools.partial(backward_kernel, scale), out_shape=[jax....  70.1 us
    pallas_call x1, Pallas kernels, forward(): pl.pallas_call(functools.partial(forward_kernel, scale), grid=(kv_heads,...  57.4 us
    pallas_call x1, Pallas kernels, finish(): pl.pallas_call(finish_kernel, out_shape=[jax.ShapeDtypeStruct(a.shape, a....  44.8 us

profile of v5, /device:TPU:1, one launch (start us, length us, event | category | flops | bytes accessed | tf_op | source)
XLA Modules:
  0.0 178.1 jit_solution(9825571525914369352)
XLA Ops:
  0.6 1.6 copy.18
  2.3 57.4 %forward.1 = (f32[64,512]{1,0:T(8,128)}, bf16[4,2,384,2176]{3,2,1,0:T(8,128)(2,1)}, bf16[4,2,384,2176]{3,2,1,0:T(8,128)(2,1)}, f32[4,2,384,1]{3,2,1,0:T(8,128)},...) custom-call(bf16[64,5120]{1,0:T(8,128)(2,1)} %bitcast.26, bf16[5120,512]{1,0:T(8,128)(2,1)} %kw_ref.3, ...), custom_call_target="tpu_custom_call" | custom-call | tf_op jit(solution)/shard_map/forward/pallas_call | solution.py:445
  59.7 70.1 %backward.1 = (f32[1,1]{1,0:T(1,128)}, bf16[96,4096]{1,0:T(8,128)(2,1)}, bf16[2,96,512]{2,1,0:T(8,128)(2,1)}, bf16[64,2560]{1,0:T(8,128)(2,1)}, f32[80,2,512]{2,1,0:T(2,128)}) custom-call(f32[96,1]{1,0:T(8,128)} %get-tuple-element.20.token_ref, s32[8]{0:T(128)} %bitcast.34, s32[8]{0:T(128)} %bitcast.35, f32[1,256]{1,0:T(1,128)} %ref_ref.1, ...), custom_call_target="tpu_custom_call" | custom-call | tf_op jit(solution)/shard_map/backward/pallas_call | solution.py:888
  129.8 44.8 %finish.1 = (bf16[96,4096]{1,0:T(8,128)(2,1)}, bf16[64,2560]{1,0:T(8,128)(2,1)}, f32[80,2,512]{2,1,0:T(2,128)}) custom-call(bf16[96,4096]{1,0:T(8,128)(2,1)} %get-tuple-element.28.refs_0_, bf16[64,2560]{1,0:T(8,128)(2,1)} %get-tuple-element.29.refs_1_, f32[80,2,512]{2,1,0:T(2,128)} %get-tuple-element.30.refs_2_), custom_call_target="tpu_custom_call" | custom-call | tf_op jit(solution)/shard_map/finish/pallas_call | solution.py:967
  174.6 1.8 %copy.16 = bf16[1,96,2,512]{3,2,1,0:T(2,128)(2,1)} copy(bf16[1,96,2,512]{3,1,2,0:T(8,128)(2,1)} %bitcast.30) | data formatting | bytes 393216

commit v6 on v3

--- a/solution.py
+++ b/solution.py
@@ -950,6 +950,24 @@
     )
 
 
+def finish_kernel(*refs):
+    count = len(refs) // 2
+    for i in range(count):
+        refs[count + i][...] = refs[i][...]
+
+
+def finish(*arrays):
+    vmem = pl.BlockSpec(memory_space=pltpu.VMEM)
+    return pl.pallas_call(
+        finish_kernel,
+        out_shape=[jax.ShapeDtypeStruct(a.shape, a.dtype) for a in arrays],
+        in_specs=[vmem] * len(arrays),
+        out_specs=[vmem] * len(arrays),
+        compiler_params=params(60),
+        name="finish",
+    )(*arrays)
+
+
 def shards(
     prompt_hidden,
     key_weight,
@@ -1011,6 +1029,7 @@
         qk_scale,
         model_width // n_ctx // 2,
     )
+    query_grad, prompt_grad, weight_grad = finish(query_grad, prompt_grad, weight_grad)
     return (
         dpo_loss.reshape(1),
         query_grad[None],

time: 138 us -> 135 us (0.978)
  local copies, waits for them, and re-layouts: 8.93 us -> 3.43 us
  Pallas kernels: 126 us -> 129 us
    unnamed x5 -> x2, local copies, waits for them, and re-layouts: 8.93 us -> 3.43 us
    pallas_call x0 -> x1, Pallas kernels: none -> 2.42 us  [finish(): pl.pallas_call(finish_kernel, out_shape=[jax.ShapeDtypeStruct(a.shape, a....]
where the time goes in v6:
time: 135 us; the launch traced here: 134 us
  Pallas kernels  129 us (96%)
  local copies, waits for them, and re-layouts  3.43 us (3%)
  between operations  2.48 us (2%)
    pallas_call x1, Pallas kernels, backward(): pl.pallas_call(functools.partial(backward_kernel, scale), out_shape=[jax....  66.1 us
    pallas_call x1, Pallas kernels, project_and_gather(): pl.pallas_call(project_kernel, out_shape=[jax.ShapeDtypeStruct((rows, wid...  33.4 us
    pallas_call x1, Pallas kernels, attend(): pl.pallas_call(functools.partial(attend_kernel, scale), grid=(kv_heads, s...  26.6 us
    unnamed x2, local copies, waits for them, and re-layouts  3.43 us

profile of v6, /device:TPU:1, one launch (start us, length us, event | category | flops | bytes accessed | tf_op | source)
XLA Modules:
  0.0 134.4 jit_solution(11027384655494991614)
XLA Ops:
  0.6 1.6 %copy.18 = bf16[1,96,2,512]{3,1,2,0:T(8,128)(2,1)} copy(bf16[1,96,2,512]{3,2,1,0:T(2,128)(2,1)} %param.15) | data formatting | bytes 393216 | tf_op args[5]
  2.3 33.4 %project_and_gather.1 = (f32[64,512]{1,0:T(8,128)}, bf16[4,4,2,64,512]{4,3,2,1,0:T(8,128)(2,1)}, bf16[4,4,2,64,512]{4,3,2,1,0:T(8,128)(2,1)}) custom-call(bf16[64,5120]{1,0:T(8,128)(2,1)} %bitcast.23, bf16[5120,512]{1,0:T(8,128)(2,1)} %kw_ref.3, bf16[5120,512]{1,0:T(8,128)(2,1)} %vw_ref.3, f32[1,128]{1,0:T(1,128)} %bitcast.29), custom_call_target="tpu_custom_call" | custom-call | tf_op jit(solution)/shard_map/project_and_gather/pallas_call | solution.py:250
  35.7 26.6 %attend.1 = (bf16[4,768,2176]{2,1,0:T(8,128)(2,1)}, bf16[4,768,2176]{2,1,0:T(8,128)(2,1)}, f32[4,768,1]{2,1,0:T(8,128)}, bf16[96,4096]{1,0:T(8,128)(2,1)}, f32[9...) custom-call(bf16[96,4096]{1,0:T(8,128)(2,1)} %bitcast.19, bf16[96,4096]{1,0:T(8,128)(2,1)} %bitcast.21, ...), custom_call_target="tpu_custom_call" | custom-call | tf_op jit(solution)/shard_map/attend/pallas_call | solution.py:455
  62.3 66.1 %backward.1 = (f32[1,1]{1,0:T(1,128)}, bf16[96,4096]{1,0:T(8,128)(2,1)}, bf16[2,96,512]{2,1,0:T(8,128)(2,1)}, bf16[64,2560]{1,0:T(8,128)(2,1)}, f32[80,2,512]{2,1,0:T(2,128)}) custom-call(f32[96,1]{1,0:T(8,128)} %get-tuple-element.24.token_ref, s32[8]{0:T(128)} %bitcast.32, s32[8]{0:T(128)} %bitcast.33, f32[1,256]{1,0:T(1,128)} %ref_ref.1, ...), custom_call_target="tpu_custom_call" | custom-call | tf_op jit(solution)/shard_map/backward/pallas_call | solution.py:887
  128.4 2.4 %finish.1 = (bf16[96,4096]{1,0:T(8,128)(2,1)}, bf16[64,2560]{1,0:T(8,128)(2,1)}, f32[80,2,512]{2,1,0:T(2,128)}) custom-call(bf16[96,4096]{1,0:T(8,128)(2,1)} %get-tuple-element.32.refs_0_, bf16[64,2560]{1,0:T(8,128)(2,1)} %get-tuple-element.33.refs_1_, f32[80,2,512]{2,1,0:T(2,128)} %get-tuple-element.34.refs_2_), custom_call_target="tpu_custom_call" | custom-call | tf_op jit(solution)/shard_map/finish/pallas_call | solution.py:961
  130.8 1.8 %copy.16 = bf16[1,96,2,512]{3,2,1,0:T(2,128)(2,1)} copy(bf16[1,96,2,512]{3,1,2,0:T(8,128)(2,1)} %bitcast.28) | data formatting | bytes 393216
